TPU v7x, 256 devices: a whole 4x4x8 slice. The times are simulated.
256 devices in a mesh: pos: 4 (over y), vocab: 64 (over z, x, core).
Axes of the slice: x: 4, y: 4, z: 8, core: 2. Of those that a mesh axis runs over, the one named last changes fastest.
Arguments:
- quantized: bfloat16 [64, 5, 8, 4096], P('vocab', None, 'pos'), may hold values from -17 to 17
- scales: float32 [64, 5, 8, 32], P('vocab', None, 'pos'), may hold values from 0.25 to 4
- norm_gain: float32 [4096], replicated, may hold values from 0.25 to 1.75
- embed_table: bfloat16 [81920, 4096], P('vocab'), may hold values from -0.390625 to 0.390625
- counts: int32 [8], replicated, may hold values from 1 to 320, 1024 in all
- positions: int32 [64, 5, 8], P(None, None, 'pos'), may hold values from 0 to 639, as said below
Outputs:
- expected: bfloat16 [64, 5, 8, 4096], P('vocab', None, 'pos')
- margins: float32 [8, 640], P('pos', 'vocab')
Inputs may be any that keep to these rules, and one draw needn't show every extreme that they name: The counts of the 8 sequences sum to 1024; the largest is 320. Within each sequence the positions of its slots are distinct and rise with the slot number j = r * 64 + v.
All inputs are finite; a program needn't handle non-finite values.
Results may differ from a plain program's by a relative error of at most 0.011.
Values may be sent and summed in bfloat16 or wider, within the bound.
A program may use at most 128 MiB of HBM per device.

v0:
```python
import math

import jax
import jax.numpy as jnp
from jax import lax
from jax.sharding import PartitionSpec as P

LEN_DEV = 10


def merged(part, axis, combine):
    gathered = jax.tree.map(lambda a: lax.all_gather(a, axis), part)

    def take(source):
        return jax.tree.map(lambda a: lax.dynamic_index_in_dim(a, source, 0, False), gathered)

    return lax.fori_loop(
        1, lax.axis_size(axis), lambda source, state: combine(state, take(source)), take(0)
    )


def pair_combine(earlier, later):
    upper = jnp.maximum(earlier[0], later[0])
    runner = jnp.maximum(jnp.minimum(earlier[0], later[0]), jnp.maximum(earlier[1], later[1]))
    return (upper, runner)


def local_leaders(logits):
    leading = jnp.max(logits, axis=-1)
    where_top = jnp.argmax(logits, axis=-1)
    vocab_ids = lax.broadcasted_iota(jnp.int32, logits.shape, logits.ndim - 1)
    runner = jnp.max(jnp.where(vocab_ids == where_top[..., None], -jnp.inf, logits), axis=-1)
    return (leading, runner)


def readout(row_block, embed_table):
    logits = jnp.einsum(
        "kmd,vd->kmv",
        lax.all_gather(row_block, "vocab", axis=0, tiled=True),
        embed_table,
        preferred_element_type=jnp.float32,
    )
    leading, runner = local_leaders(logits)
    top_one, top_two = merged((leading, runner), "vocab", pair_combine)
    softmax_sum = lax.psum(jnp.sum(jnp.exp(logits - top_one[..., None]), axis=-1), "vocab")
    weights_soft = (jnp.exp(logits - top_one[..., None]) / softmax_sum[..., None]).astype(
        jnp.bfloat16
    )
    mixture = lax.psum_scatter(
        jnp.einsum("kmv,vd->kmd", weights_soft, embed_table, preferred_element_type=jnp.float32),
        "vocab",
        scatter_dimension=0,
        tiled=True,
    )
    mixture = mixture * math.sqrt(embed_table.shape[1])
    margin_rows = (1.0 - jnp.exp(top_two - top_one)) / softmax_sum
    return (mixture, margin_rows)


def on_device(quantized, scales, norm_gain, embed_table, counts, positions):
    col_count = lax.axis_size("vocab")
    col_index = lax.axis_index("vocab")
    grp_index = lax.axis_index("pos")
    slot_rows = quantized.shape[1]
    grp_seqs = quantized.shape[2]
    model_width = quantized.shape[3]
    dequant = (
        quantized.astype(jnp.float32).reshape(1, slot_rows, grp_seqs, model_width // 128, 128)
        * scales[..., None]
    )
    dequant = dequant.reshape(1, slot_rows, grp_seqs, model_width)
    square_mean = jnp.mean(dequant * dequant, axis=-1, keepdims=True)
    normed = (dequant * lax.rsqrt(square_mean + 1e-06) * norm_gain).astype(jnp.bfloat16)
    own_rows = normed.reshape(1, slot_rows * grp_seqs, model_width)
    group_counts = lax.dynamic_slice_in_dim(counts, grp_index * grp_seqs, grp_seqs)
    row_id = jnp.arange(slot_rows, dtype=jnp.int32)[:, None]
    own_live = row_id * col_count + col_index < group_counts[None, :]
    column_ids = jnp.arange(col_count, dtype=jnp.int32)[:, None, None]
    group_live = column_ids + row_id[None] * col_count < group_counts[None, None, :]
    mixture, margin_rows = readout(own_rows, embed_table)
    own_mixture = mixture.reshape(1, slot_rows, grp_seqs, model_width)
    group_margins = margin_rows.reshape(col_count, slot_rows, grp_seqs)
    expected = jnp.where(own_live[None, :, :, None], own_mixture, 0.0).astype(jnp.bfloat16)
    group_margins = jnp.where(group_live, group_margins, 0.0)
    targets = col_index * LEN_DEV + jnp.arange(LEN_DEV, dtype=jnp.int32)
    position_hits = positions[..., None] == targets
    margins = jnp.sum(jnp.where(position_hits, group_margins[..., None], 0.0), axis=(0, 1))
    return (expected, margins)


def solution(mesh):
    in_specs = (
        P("vocab", None, "pos", None),
        P("vocab", None, "pos", None),
        P(),
        P("vocab", None),
        P(),
        P(None, None, "pos"),
    )
    out_specs = (P("vocab", None, "pos", None), P("pos", "vocab"))
    return jax.shard_map(
        on_device, mesh=mesh, in_specs=in_specs, out_specs=out_specs, check_vma=False
    )
```

profile of v0, /device:TPU:16, one launch (start us, length us, event | category | flops | bytes accessed | tf_op | source)
XLA Modules:
  0.0 617.7 jit_solution(5096089379869772827)
XLA Ops:
  7.2 0.8 mul.74
  8.1 1.1 multiply_reduce_fusion
  9.2 1.0 multiply_convert_fusion
  11.0 85.9 %all-gather.6.cloned.1.call-done = bf16[64,10,4096]{2,1,0:T(8,128)(2,1)} async-done(((bf16[1,10,4096]{2,1,0:T(8,128)(2,1)}), bf16[64,10,4096]{2,1,0:T(8,128)(2,1)}) %all-gather.6.cloned.1.call-update) | async-done | bytes 5242896 | tf_op jit(solution)/shard_map/all_gather | solution.py:39
  96.9 15.9 %fusion.3 = f32[64,10,1280]{2,0,1:T(8,128)S(1)} fusion(bf16[1280,4096]{1,0:T(8,128)(2,1)} %param.11, bf16[64,10,4096]{2,1,0:T(8,128)(2,1)} %all-gather.6.cloned.1.call-done), kind=kOutput, calls=%fused_computation.6 | convolution fusion | flops 6710886400 | bytes 19005440 | tf_op jit(solution)/shard_map/kmd,vd->kmv/dot_general | solution.py:37
  112.8 1.6 iota_reduce_fusion
  115.0 49.5 %all-gather.3 = f32[64,64,10]{1,2,0:T(8,128)S(1)} all-gather(f32[1,64,10]{1,2,0:T(8,128)S(1)} %bitcast.33), channel_id=3, replica_groups=mesh['pos'=4,'vocab'=64] {'vocab'}, dimensions={0}, use_global_device_ids=true | all-gather | bytes 166400 | tf_op jit(solution)/shard_map/all_gather | solution.py:12
  164.5 48.0 %all-gather.2 = f32[64,64,10]{1,2,0:T(8,128)S(1)} all-gather(f32[1,64,10]{1,2,0:T(8,128)S(1)} %bitcast.32), channel_id=2, replica_groups=mesh['pos'=4,'vocab'=64] {'vocab'}, dimensions={0}, use_global_device_ids=true | all-gather | bytes 166400 | tf_op jit(solution)/shard_map/all_gather | solution.py:12
  212.4 0.8 copy-done.1
  213.2 45.4 %while.17 = (s32[]{:T(128)}, f32[64,10]{0,1:T(8,128)S(1)}, f32[64,10]{0,1:T(8,128)S(1)}, f32[64,64,10]{1,2,0:T(8,128)}, f32[64,64,10]{1,2,0:T(8,128)}, /*index=5*/s32[]{:T(128)}, s32[]{:T(128)}, s32[]{:T(128)}) while((s32[]{:T(128)}, f32[64,10]{0,1:T(8,128)S(1)}, f32[64,10]{0,1:T(8,128)S(1)}, f32[64,64,10]{1,2,0:T(8,128)}, ...), condition=%wide.region_4.5_spmd, body=%wide.region_3.4_spmd.sunk | while | flops 2565 | bytes 15483 | solution.py:17
  213.2 0.7 fusion.12
  213.9 0.7 fusion.12
  216.8 0.7 fusion.12
  236.3 0.7 fusion.12
  237.0 0.7 fusion.12
  253.6 0.7 fusion.12
  254.3 0.7 fusion.12
  255.0 0.8 fusion.12
  257.9 0.7 fusion.12
  259.3 128.7 %psum.7 = f32[64,10]{0,1:T(8,128)S(1)} all-reduce(f32[64,10]{0,1:T(8,128)S(1)} %fusion.6), channel_id=1, replica_groups=mesh['pos'=4,'vocab'=64] {'vocab'}, use_global_device_ids=true, to_apply=%region_6.7 | all-reduce | flops 640 | bytes 5120 | tf_op jit(solution)/shard_map/psum | solution.py:45
  388.0 12.6 %fusion.1 = f32[64,10,4096]{2,0,1:T(8,128)} fusion(bf16[1280,4096]{1,0:T(8,128)(2,1)} %param.11, f32[64,10,1280]{2,0,1:T(8,128)S(1)} %fusion.3, f32[64,10]{0,1:T(8,128)S(1)} %psum.7, f32[64,10]{0,1:T(8,128)S(1)} %get-tuple-element.140), kind=kOutput, calls=%fused_computation.4 | convolution fusion | flops 6713344000 | bytes 24253440 | tf_op jit(solution)/shard_map/kmv,vd->kmd/dot_general | solution.py:50
  403.0 204.9 %all-reduce.3.cloned.1.call-done = f32[64,10,4096]{2,0,1:T(8,128)} async-done(((f32[64,10,4096]{2,0,1:T(8,128)}), f32[64,10,4096]{2,0,1:T(8,128)}) %all-reduce.3.cloned.1.call-update) | async-done | bytes 10485776
  607.9 2.1 dynamic-slice_multiply_fusion
  610.0 0.8 fusion.9
  (86 shorter events, 43.3 us)
Async XLA Ops:
  7.2 89.7 %all-gather.6.cloned.1.call-start = ((), (), s32[]{:S(2)}) async-start(), calls=%async_computation | async-start | bytes 8519680 | tf_op jit(solution)/shard_map/all_gather | solution.py:39
  10.9 596.9 %all-reduce.3.cloned.1.call-start = ((), (), s32[]{:S(2)}) async-start(), calls=%async_computation.1 | async-start | bytes 20971520
  164.5 48.0 %copy-start = (f32[64,64,10]{1,2,0:T(8,128)}, f32[64,64,10]{1,2,0:T(8,128)S(1)}, u32[]{:S(2)}) copy-start(f32[64,64,10]{1,2,0:T(8,128)S(1)} %all-gather.3) | copy-start | bytes 491524
  212.4 0.8 copy-start.1
  400.6 0.7 copy-start.4
  400.6 1.3 copy-start.3
  400.6 1.6 copy-start.2
Sparse Core Ops, SparseCore 0:
  11.1 85.7 all-gather.5
  400.7 207.1 all-reduce.2
where the time goes:
time: 625 us; the launch traced here: 618 us
  waiting for transfers between devices  291 us (47%)
  blocking collectives  226 us (36%)
  other arithmetic  53.7 us (9%)
  matrix products  28.5 us (5%)
  between operations  14.1 us (2%)
    unnamed x3, waiting for transfers between devices  205 us
    psum x1, blocking collectives, readout(): lax.psum(jnp.sum(jnp.exp(logits - top_one[..., None]), axis=-1), 'vocab')  129 us
    all_gather x2, blocking collectives, merged(): gathered = jax.tree.map(lambda a: lax.all_gather(a, axis), part)  97.4 us
    all_gather x1, waiting for transfers between devices, readout(): lax.all_gather(row_block, 'vocab', axis=0, tiled=True)  85.9 us
    max x63, other arithmetic, pair_combine(): jnp.maximum(jnp.minimum(earlier[0], later[0]), jnp.maximum(earlier[1], la...  45.4 us
    dot_general x1, matrix products, readout(): jnp.einsum('kmd,vd->kmv', lax.all_gather(row_block, 'vocab', axis=0, tile...  15.9 us
    dot_general x1, matrix products, readout(): jnp.einsum('kmv,vd->kmd', weights_soft, embed_table, preferred_element_ty...  12.6 us
  transfers between devices with their start and end apart: 2, of which 2 were waited for; matrix products, arithmetic and copies ran while one was open for 0% of the time, Pallas kernels for 0%

commit v1 on v0

v1 whole, which is shorter than its diff:
```python
import functools

import jax
import jax.numpy as jnp
from jax import lax
from jax.experimental import pallas as pl
from jax.experimental.pallas import tpu as pltpu
from jax.sharding import PartitionSpec as P

MESH = pl.DeviceIdType.MESH
F32 = jnp.float32
BF16 = jnp.bfloat16

D = 4096
LEN_DEV = 10
NY, NZ, NX, NC = 4, 8, 4, 2
NK = NX * NC
CAPR = 6
ROWS = NK * CAPR
M = NK * ROWS
V = 1280
H = 2
DH = D // H
CW = DH // NK
SLOTS = 10
SP = 16


def onehot(cond):
    return jnp.where(cond, 1.0, 0.0).astype(BF16)


def iota(shape, dim):
    return lax.broadcasted_iota(jnp.int32, shape, dim)


def div48(i):
    return lax.shift_right_logical(i * 683, 15)


def div6(i):
    return lax.shift_right_logical(i * 43, 8)


def merge(parts):
    top = functools.reduce(jnp.maximum, [p[0] for p in parts])
    total = sum(p[2] * jnp.exp(p[0] - top) for p in parts)
    m1, m2 = parts[0][0], parts[0][1]
    for p in parts[1:]:
        m2 = jnp.maximum(jnp.minimum(m1, p[0]), jnp.maximum(m2, p[1]))
        m1 = jnp.maximum(m1, p[0])
    return m1, m2, total


def kernel(
    q_ref, sc_ref, gain_ref, e_hbm, cnt_ref,
    out_ref, marg_ref,
    e_v, xcat, sb, yr, g, perm, x_v, l_v, p_v, tt, fsc, o32, obf, cr, xs, xr, pst, zs, zr, ys, yr2,
    st_c, st_x, st_z, st_o,
    esem, ysend, yrecv, zsend, zrecv, xsend, xrecv, csend, crecv,
    c2send, c2recv, x2send, x2recv, z2send, z2recv, y2send, y2recv,
    scs, scr, sxs, sxr, szs, szr, ms, mr,
):
    y = lax.axis_index("pos")
    v = lax.axis_index("vocab")
    z = v // NK
    k = lax.rem(v, NK)
    x = k // NC
    c = lax.rem(k, NC)

    def dev(yy, zz, xx, cc):
        return (yy, zz * NK + xx * NC + cc)

    def ypart(o):
        return dev(lax.rem(y + o, NY), z, x, c)

    def zpart(o):
        return dev(y, lax.rem(z + o, NZ), x, c)

    def xpart(o):
        return dev(y, z, lax.rem(x + o, NX), c)

    cpart = dev(y, z, x, 1 - c)
    yoffs, zoffs, xoffs = (1, 3, 2), (4, 3, 5, 2, 6, 1, 7), (2, 1, 3)
    pending = []

    def send(src, dst, ss, rs, to):
        cp = pltpu.make_async_remote_copy(
            src_ref=src, dst_ref=dst, send_sem=ss, recv_sem=rs, device_id=to, device_id_type=MESH
        )
        cp.start()
        pending.append(cp)
        return cp

    def blk(kk):
        return pl.ds(pl.multiple_of(kk * ROWS, 16), ROWS)

    barrier = pltpu.get_barrier_semaphore()
    partners = [ypart(o) for o in yoffs] + [zpart(o) for o in zoffs]
    partners += [xpart(o) for o in xoffs] + [cpart]
    for to in partners:
        pl.semaphore_signal(barrier, inc=1, device_id=to, device_id_type=MESH)
    e_copy = pltpu.make_async_copy(e_hbm, e_v, esem)
    e_copy.start()

    q = q_ref[...].astype(F32)
    sc = sc_ref[...]
    deq = [q[:, i * 128:(i + 1) * 128] * sc[:, i:i + 1] for i in range(D // 128)]
    sq = sum(d * d for d in deq)
    inv = lax.rsqrt(jnp.sum(sq, axis=1, keepdims=True) * (1.0 / D) + 1e-6)
    xcat[...] = jnp.zeros_like(xcat)
    for i in range(D // 128):
        h, rest = divmod(i * 128, DH)
        cc, lane = divmod(rest, CW)
        gn = gain_ref[:, i * 128:(i + 1) * 128]
        row = (deq[i] * inv * gn).astype(BF16)
        xcat[h, cc * SP:cc * SP + SLOTS, lane:lane + 128] = row

    before = []
    run = jnp.int32(0)
    for s in range(8):
        before.append(run)
        run = run + lax.shift_right_logical(cnt_ref[s] + 63, 6)
    bars = []
    for r5 in range(5):
        for s2 in range(2):
            seq = y * 2 + s2
            first = jnp.int32(0)
            for s in range(8):
                first = jnp.where(seq == s, before[s], first)
            bars.append(jnp.where(r5 * 64 + v < cnt_ref[seq], first + r5, -1))

    def slot_bar(j):
        bar = jnp.full(j.shape, -1, jnp.int32)
        for i, b in enumerate(bars):
            bar = jnp.where(j == i, b, bar)
        return bar

    shape = (NY * ROWS, NK * SP)
    i0 = iota((NY * ROWS, 1), 0)
    o_i = div48(i0)
    ci = div6(i0 - o_i * ROWS)
    ri = i0 - o_i * ROWS - ci * CAPR
    want = ri * NY + jnp.bitwise_and(y + o_i, NY - 1)
    j0 = iota((1, NK * SP), 1)
    cj = lax.shift_right_logical(j0, 4)
    bar_j = slot_bar(jnp.bitwise_and(j0, SP - 1))
    pick = onehot(
        (jnp.broadcast_to(ci, shape) == jnp.broadcast_to(cj, shape))
        & (jnp.broadcast_to(want, shape) == jnp.broadcast_to(bar_j, shape))
    )
    for h in range(H):
        blocks = jnp.dot(pick, xcat[h], preferred_element_type=F32).astype(BF16)
        for o in range(NY):
            sb[h, o] = blocks[o * ROWS:(o + 1) * ROWS]

    pl.semaphore_wait(barrier, len(partners))

    ycp = {}
    for h in range(H):
        for o in yoffs:
            ycp[h, o] = send(sb.at[h, o], yr.at[h, o], ysend.at[h, o], yrecv.at[h, o], ypart(o))

    pi = iota((M, 1), 0)
    pa = div48(pi)
    pb = div6(pi - pa * ROWS)
    pr = pi - pa * ROWS - pb * CAPR
    perm[...] = onehot(
        jnp.broadcast_to(pb * ROWS + pa * CAPR + pr, (M, M)) == iota((M, M), 1)
    )

    zcp = {}
    for h in range(H):
        for o in yoffs:
            ycp[h, o].wait_recv()
        own = sb[h, 0].astype(F32)
        for o in yoffs:
            own = own + yr[h, o].astype(F32)
        g[h, blk(z), :] = own.astype(BF16)
        for o in zoffs:
            zcp[h, o] = send(
                g.at[h, blk(z)], g.at[h, blk(z)], zsend.at[h, o], zrecv.at[h, o], zpart(o)
            )

    xcp, ccp = {}, {}

    def half(ref, rows, h):
        return ref.at[rows, pl.ds(h * DH, DH)]

    for h in range(H):
        for o in zoffs:
            zcp[h, o].wait_recv()
        lines = jnp.dot(perm[...], g[h], preferred_element_type=F32).astype(BF16)
        for cc in range(NK):
            x_v[blk(k), h * DH + cc * CW:h * DH + (cc + 1) * CW] = lines[cc * ROWS:(cc + 1) * ROWS]
        mine = half(x_v, blk(k), h)
        for o in xoffs:
            xcp[h, o] = send(mine, mine, xsend.at[h, o], xrecv.at[h, o], xpart(o))
        ccp[h, 0] = send(mine, mine, csend.at[h, 0], crecv.at[h, 0], cpart)

    for h in range(H):
        for o in (1, 3, 2):
            xcp[h, o].wait_recv()
            got = half(x_v, blk(lax.rem(x + NX - o, NX) * NC + c), h)
            ccp[h, o] = send(got, got, csend.at[h, o], crecv.at[h, o], cpart)
        for o in (0, 1, 3, 2):
            ccp[h, o].wait_recv()
        if h == 0:
            e_copy.wait()

        def mm1(i, carry):
            n = pl.ds(pl.multiple_of(i * 256, 256), 256)
            part = lax.dot_general(
                x_v[:, h * DH:(h + 1) * DH], e_v[n, h * DH:(h + 1) * DH],
                (((1,), (1,)), ((), ())), preferred_element_type=F32,
            )
            l_v[:, n] = part if h == 0 else l_v[:, n] + part
            return carry

        lax.fori_loop(0, V // 256, mm1, 0)

    def stats(i, carry):
        r = pl.ds(pl.multiple_of(i * 128, 128), 128)
        t1 = l_v[r, 0:128]
        t2 = jnp.full((128, 128), -jnp.inf, F32)
        for j in range(1, V // 128):
            val = l_v[r, j * 128:(j + 1) * 128]
            t2 = jnp.maximum(t2, jnp.minimum(t1, val))
            t1 = jnp.maximum(t1, val)
        top = jnp.max(t1, axis=1, keepdims=True)
        acc = jnp.zeros((128, 128), F32)
        for j in range(V // 128):
            e = jnp.exp(l_v[r, j * 128:(j + 1) * 128] - top)
            acc = acc + e
            p_v[r, j * 128:(j + 1) * 128] = e.astype(BF16)
        tt[0, :, r] = t1.T
        tt[1, :, r] = t2.T
        tt[2, :, r] = acc.T
        return carry

    for i in range(M // 128):
        stats(i, 0)
    m1, m2, sm = tt[0], tt[1], tt[2]
    n = 128
    while n > 1:
        n //= 2
        a1, b1 = m1[:n], m1[n:]
        m2 = jnp.maximum(jnp.minimum(a1, b1), jnp.maximum(m2[:n], m2[n:]))
        m1 = jnp.maximum(a1, b1)
        sm = sm[:n] + sm[n:]
    loc = m1

    def put(slot, parts):
        st_o[slot, 0:1] = parts[0]
        st_o[slot, 1:2] = parts[1]
        st_o[slot, 2:3] = parts[2]

    def got3(ref):
        return (ref[0:1], ref[1:2], ref[2:3])

    def mm2(h, lo, hi):
        def body(i, carry):
            n = pl.ds(pl.multiple_of(h * DH + i * 256, 256), 256)
            o32[:, n] = jnp.dot(p_v[...], e_v[:, n], preferred_element_type=F32)
            return carry

        lax.fori_loop(lo, hi, body, 0)

    half_n = DH // 512
    st_o[...] = jnp.zeros_like(st_o)
    cur = (m1, m2, sm)
    put(0, cur)
    cp = send(st_o.at[0], st_c, scs, scr, cpart)
    mm2(0, 0, half_n)
    cp.wait_recv()
    cur = merge([cur, got3(st_c)])
    put(1, cur)
    cps = [send(st_o.at[1], st_x.at[o], sxs.at[o], sxr.at[o], xpart(o)) for o in xoffs]
    mm2(0, half_n, 2 * half_n)
    for cp in cps:
        cp.wait_recv()
    cur = merge([cur] + [got3(st_x[o]) for o in xoffs])
    put(2, cur)
    cps = [send(st_o.at[2], st_z.at[o], szs.at[o], szr.at[o], zpart(o)) for o in zoffs]
    mm2(1, 0, half_n)
    for cp in cps:
        cp.wait_recv()
    m1, m2, sm = merge([cur] + [got3(st_z[o]) for o in zoffs])
    factor = jnp.exp(loc - m1) / sm * 64.0
    for i in range(M // 128):
        fsc[i * 128:(i + 1) * 128] = jnp.broadcast_to(factor[:, i * 128:(i + 1) * 128], (128, 128)).T
    margin = (1.0 - jnp.exp(m2 - m1)) / sm
    marg_ref[y] = jnp.broadcast_to(margin, (8, M))
    mcp = [send(marg_ref.at[y], marg_ref.at[y], ms.at[o], mr.at[o], ypart(o)) for o in yoffs]

    def scale(h):
        def body(i, carry):
            n = pl.ds(pl.multiple_of(h * DH + i * 128, 128), 128)
            obf[:, n] = (o32[:, n] * fsc[...]).astype(BF16)
            return carry

        lax.fori_loop(0, DH // 128, body, 0)

    c2, x2, z2, y2 = {}, {}, {}, {}

    def core_send(h):
        for o in (2, 1, 3, 0):
            xx = lax.rem(x + o, NX)
            c2[h, o] = send(
                half(obf, blk(xx * NC + 1 - c), h), cr.at[h, o], c2send.at[h, o], c2recv.at[h, o], cpart
            )

    scale(0)
    core_send(0)
    mm2(1, half_n, 2 * half_n)
    scale(1)
    core_send(1)
    for h in range(H):
        for o in (2, 1, 3, 0):
            c2[h, o].wait_recv()
            mine = obf[blk(lax.rem(x + o, NX) * NC + c), h * DH:(h + 1) * DH]
            xs[h, o] = (mine.astype(F32) + cr[h, o].astype(F32)).astype(BF16)
            if o:
                x2[h, o] = send(xs.at[h, o], xr.at[h, o], x2send.at[h, o], x2recv.at[h, o], xpart(o))
    for h in range(H):
        for o in xoffs:
            x2[h, o].wait_recv()
        for cc in range(NK):
            ln = slice(cc * CW, (cc + 1) * CW)
            tot = xs[h, 0, :, ln].astype(F32)
            for o in xoffs:
                tot = tot + xr[h, o, :, ln].astype(F32)
            pst[cc * ROWS:(cc + 1) * ROWS] = tot.astype(BF16)
        zs[h] = jnp.dot(perm[...], pst[...], preferred_element_type=F32).astype(BF16)
        for o in zoffs:
            z2[h, o] = send(
                zs.at[h, blk(lax.rem(z + o, NZ))], zr.at[h, o], z2send.at[h, o], z2recv.at[h, o], zpart(o)
            )
    for h in range(H):
        for o in zoffs:
            z2[h, o].wait_recv()
        tot = zs[h, blk(z), :].astype(F32)
        for o in zoffs:
            tot = tot + zr[h, o].astype(F32)
        ys[h] = tot.astype(BF16)
        yr2[h, 0] = ys[h]
        for o in yoffs:
            y2[h, o] = send(ys.at[h], yr2.at[h, o], y2send.at[h, o], y2recv.at[h, o], ypart(o))

    shape = (NK * SP, NY * ROWS)
    j0 = iota((1, NY * ROWS), 1)
    o_j = div48(j0)
    cj = div6(j0 - o_j * ROWS)
    rj = j0 - o_j * ROWS - cj * CAPR
    have = rj * NY + jnp.bitwise_and(y + NY - o_j, NY - 1)
    i0 = iota((NK * SP, 1), 0)
    ci = lax.shift_right_logical(i0, 4)
    bar_i = slot_bar(jnp.bitwise_and(i0, SP - 1))
    back = onehot(
        (jnp.broadcast_to(ci, shape) == jnp.broadcast_to(cj, shape))
        & (jnp.broadcast_to(bar_i, shape) == jnp.broadcast_to(have, shape))
    )
    for h in range(H):
        for o in yoffs:
            y2[h, o].wait_recv()
        cat = jnp.concatenate([yr2[h, o] for o in range(NY)], axis=0)
        res = jnp.dot(back, cat, preferred_element_type=F32).astype(BF16)
        for cc in range(NK):
            out_ref[:, h * DH + cc * CW:h * DH + (cc + 1) * CW] = res[cc * SP:(cc + 1) * SP]

    for cp in mcp:
        cp.wait_recv()
    for cp in pending:
        cp.wait_send()


def readout(q, sc, gain, table, counts):
    dma = pltpu.SemaphoreType.DMA
    vm = pl.BlockSpec(memory_space=pltpu.VMEM)
    return pl.pallas_call(
        kernel,
        out_shape=(
            jax.ShapeDtypeStruct((SP, D), BF16),
            jax.ShapeDtypeStruct((NY, 8, M), F32),
        ),
        in_specs=[vm, vm, vm, pl.BlockSpec(memory_space=pl.ANY), pl.BlockSpec(memory_space=pltpu.SMEM)],
        out_specs=(vm, vm),
        scratch_shapes=[
            pltpu.VMEM((V, D), BF16),
            pltpu.VMEM((H, NK * SP, CW), BF16),
            pltpu.VMEM((H, NY, ROWS, CW), BF16),
            pltpu.VMEM((H, NY, ROWS, CW), BF16),
            pltpu.VMEM((H, M, CW), BF16),
            pltpu.VMEM((M, M), BF16),
            pltpu.VMEM((M, D), BF16),
            pltpu.VMEM((M, V), F32),
            pltpu.VMEM((M, V), BF16),
            pltpu.VMEM((3, 128, M), F32),
            pltpu.VMEM((M, 128), F32),
            pltpu.VMEM((M, D), F32),
            pltpu.VMEM((M, D), BF16),
            pltpu.VMEM((H, NX, ROWS, DH), BF16),
            pltpu.VMEM((H, NX, ROWS, DH), BF16),
            pltpu.VMEM((H, NX, ROWS, DH), BF16),
            pltpu.VMEM((M, CW), BF16),
            pltpu.VMEM((H, M, CW), BF16),
            pltpu.VMEM((H, NZ, ROWS, CW), BF16),
            pltpu.VMEM((H, ROWS, CW), BF16),
            pltpu.VMEM((H, NY, ROWS, CW), BF16),
            pltpu.VMEM((8, M), F32),
            pltpu.VMEM((NX, 8, M), F32),
            pltpu.VMEM((NZ, 8, M), F32),
            pltpu.VMEM((3, 8, M), F32),
            dma,
            dma((H, NY)), dma((H, NY)), dma((H, NZ)), dma((H, NZ)),
            dma((H, NX)), dma((H, NX)), dma((H, NX)), dma((H, NX)),
            dma((H, NX)), dma((H, NX)), dma((H, NX)), dma((H, NX)),
            dma((H, NZ)), dma((H, NZ)), dma((H, NY)), dma((H, NY)),
            dma, dma, dma((NX,)), dma((NX,)), dma((NZ,)), dma((NZ,)), dma((NY,)), dma((NY,)),
        ],
        compiler_params=pltpu.CompilerParams(
            collective_id=0, has_side_effects=True, vmem_limit_bytes=60 << 20
        ),
        cost_estimate=pl.CostEstimate(
            flops=4 * M * V * D, bytes_accessed=2 * V * D, transcendentals=M * V
        ),
        name="readout",
    )(q, sc, gain, table, counts)


def on_device(quantized, scales, norm_gain, embed_table, counts, positions):
    col = lax.axis_index("vocab")
    grp = lax.axis_index("pos")
    rows, seqs = quantized.shape[1], quantized.shape[2]
    out, marg = readout(
        quantized.reshape(SLOTS, D), scales.reshape(SLOTS, D // 128), norm_gain.reshape(1, D),
        embed_table, counts,
    )
    expected = out[:SLOTS].reshape(1, rows, seqs, D)
    by_bar = marg[:, 0].reshape(NY, NK, NZ, CAPR).transpose(3, 0, 2, 1).reshape(NY * CAPR, NZ * NK)
    filled = (counts + 63) // 64
    first = jnp.cumsum(filled) - filled
    own_first = lax.dynamic_slice_in_dim(first, grp * seqs, seqs)
    own_counts = lax.dynamic_slice_in_dim(counts, grp * seqs, seqs)
    row = jnp.arange(rows, dtype=jnp.int32)[:, None]
    bar = jnp.minimum(own_first[None] + row, NY * CAPR - 1)
    values = by_bar[bar]
    slot = row[..., None] * (NZ * NK) + jnp.arange(NZ * NK, dtype=jnp.int32)
    values = jnp.where(slot < own_counts[None, :, None], values, 0.0)
    targets = col * LEN_DEV + jnp.arange(LEN_DEV, dtype=jnp.int32)
    hits = positions.transpose(1, 2, 0)[..., None] == targets
    margins = jnp.sum(jnp.where(hits, values[..., None], 0.0), axis=(0, 2))
    return (expected, margins)


def solution(mesh):
    in_specs = (
        P("vocab", None, "pos", None),
        P("vocab", None, "pos", None),
        P(),
        P("vocab", None),
        P(),
        P(None, None, "pos"),
    )
    out_specs = (P("vocab", None, "pos", None), P("pos", "vocab"))
    return jax.shard_map(
        on_device, mesh=mesh, in_specs=in_specs, out_specs=out_specs, check_vma=False
    )
```

time: 625 us -> 96.5 us (0.15); the launches traced: 618 us -> 96 us
  waiting for transfers between devices: 291 us -> 0 us
  blocking collectives: 226 us -> 0 us
  Pallas kernels: 0 us -> 87.4 us
  other arithmetic: 53.7 us -> 0.55 us
  matrix products: 28.5 us -> 0 us
  between operations: 14.1 us -> 0.7 us
    unnamed x3 -> x0, waiting for transfers between devices: 205 us -> none
    psum x1 -> x0, blocking collectives: 129 us -> none  [readout(): lax.psum(jnp.sum(jnp.exp(logits - top_one[..., None]), axis=-1), 'vocab')]
    all_gather x2 -> x0, blocking collectives: 97.4 us -> none  [merged(): gathered = jax.tree.map(lambda a: lax.all_gather(a, axis), part)]
    pallas_call x0 -> x1, Pallas kernels: none -> 87.4 us  [readout(): pl.pallas_call(kernel, out_shape=(jax.ShapeDtypeStruct((SP, D), BF16), ja...]
    all_gather x1 -> x0, waiting for transfers between devices: 85.9 us -> none  [readout(): lax.all_gather(row_block, 'vocab', axis=0, tiled=True)]
    max x63 -> x0, other arithmetic: 45.4 us -> none  [pair_combine(): jnp.maximum(jnp.minimum(earlier[0], later[0]), jnp.maximum(earlier[1], la...]
    dot_general x2 -> x0, matrix products: 28.5 us -> none  [the longest x1 15.9 us: readout(): jnp.einsum('kmd,vd->kmv', lax.all_gather(row_block, 'vocab', axis=0, tile...]
  transfers between devices with their start and end apart: 2 -> 0, of which waited for: 2 -> 0; matrix products, arithmetic and copies ran while one was open for 0% -> 0% of each run, Pallas kernels for 0% -> 0%
where the time goes in v1:
time: 96.5 us; the launch traced here: 96 us
  Pallas kernels  87.4 us (91%)
  local copies, waits for them, and re-layouts  7.31 us (8%)
    pallas_call x1, Pallas kernels, readout(): pl.pallas_call(kernel, out_shape=(jax.ShapeDtypeStruct((SP, D), BF16), ja...  87.4 us

profile of v1, /device:TPU:16, one launch (start us, length us, event | category | flops | bytes accessed | tf_op | source)
XLA Modules:
  0.0 96.0 jit_solution(7626022061082367690)
XLA Ops:
  0.6 1.6 %reshape.122.q_ref = bf16[10,4096]{1,0:T(8,128)(2,1)} reshape(bf16[1,5,2,4096]{3,2,1,0:T(2,128)(2,1)} %param.6) | data formatting | bytes 163840 | tf_op jit(solution)/shard_map/reshape | solution.py:436
  2.2 1.3 %reshape.123.sc_ref = f32[10,32]{1,0:T(8,128)} reshape(f32[1,5,2,32]{3,2,1,0:T(2,128)} %param.7) | data formatting | bytes 2560 | tf_op jit(solution)/shard_map/reshape | solution.py:436
  3.5 0.0 copy-start.1
  3.5 0.0 copy-start
  3.5 87.4 %readout.1 = (bf16[16,4096]{1,0:T(8,128)(2,1)}, f32[4,8,384]{2,1,0:T(8,128)}) custom-call(bf16[10,4096]{1,0:T(8,128)(2,1)} %reshape.122.q_ref, f32[10,32]{1,0:T(8,128)} %reshape.123.sc_ref, f32[1,4096]{1,0:T(1,128)} %bitcast.15, bf16[1280,4096]{1,0:T(8,128)(2,1)} %e_hbm.1, s32[8]{0:T(128)} %cnt_ref.1), custom_call_target="tpu_custom_call" | custom-call | flops 8053063680 | bytes 10485760 | tf_op jit(solution)/shard_map/readout/pallas_call | solution.py:380
  90.9 1.6 %reshape.125 = bf16[1,5,2,4096]{3,2,1,0:T(2,128)(2,1)} reshape(bf16[10,4096]{1,0:T(8,128)(2,1)} %bitcast.13) | data formatting | bytes 163840 | tf_op jit(solution)/shard_map/reshape | solution.py:439
  92.6 0.8 slice_reduce_fusion
  93.4 0.1 reshape_squeeze.3
  93.5 0.3 copy.10
  93.9 0.1 reshape.126
  94.0 0.0 copy-done.1
  94.0 0.2 reduce-window.9
  94.2 0.1 dynamic_slice.7
  94.3 0.1 reshape.131
  94.4 0.6 gather_fusion
  95.0 0.1 iota_add_fusion
  95.0 0.1 dynamic_slice.6
  95.1 0.1 compare_select_fusion.2
  95.2 0.0 copy-done
  95.2 0.2 fusion
  95.4 0.7 copy.11
  (7 shorter events, 0.1 us)
Async XLA Ops:
  3.5 90.5 %copy-start.1 = (s32[8]{0:T(128)S(1)}, s32[8]{0:T(128)}, u32[]{:S(2)}) copy-start(s32[8]{0:T(128)} %cnt_ref.1) | copy-start | bytes 100
  3.5 91.7 %copy-start = (s32[64,5,2]{0,2,1:T(2,128)S(1)}, s32[64,5,2]{0,2,1:T(2,128)}, u32[]{:S(2)}) copy-start(s32[64,5,2]{0,2,1:T(2,128)} %param.11) | copy-start | bytes 7684

commit v2 on v1

v2 whole, which is shorter than its diff:
```python
import functools

import jax
import jax.numpy as jnp
from jax import lax
from jax.experimental import pallas as pl
from jax.experimental.pallas import tpu as pltpu
from jax.sharding import PartitionSpec as P

MESH = pl.DeviceIdType.MESH
F32 = jnp.float32
BF16 = jnp.bfloat16

D = 4096
LEN_DEV = 10
NY, NZ, NX, NC = 4, 8, 4, 2
NK = NX * NC
CAPR = 6
ROWS = NK * CAPR
GR = NZ * ROWS
LR = 32
OVR = 2
MAIN = NK * LR
OV = NK * OVR
M = MAIN + OV
ML = 384
V = 1280
H = 2
DH = D // H
CW = DH // NK
SLOTS = 10
SP = 16
BARS = 40


def onehot(cond):
    return jnp.where(cond, 1.0, 0.0).astype(BF16)


def iota(shape, dim):
    return lax.broadcasted_iota(jnp.int32, shape, dim)


def div48(i):
    return lax.shift_right_logical(i * 683, 15)


def div6(i):
    return lax.shift_right_logical(i * 43, 8)


def count(cond, axis):
    return jnp.sum(jnp.where(cond, 1.0, 0.0), axis=axis, keepdims=True).astype(jnp.int32)


def merge(parts):
    top = functools.reduce(jnp.maximum, [p[0] for p in parts])
    total = sum(p[2] * jnp.exp(p[0] - top) for p in parts)
    m1, m2 = parts[0][0], parts[0][1]
    for p in parts[1:]:
        m2 = jnp.maximum(jnp.minimum(m1, p[0]), jnp.maximum(m2, p[1]))
        m1 = jnp.maximum(m1, p[0])
    return m1, m2, total


def kernel(
    q_ref, sc_ref, gain_ref, e_hbm, cnt_ref, pos_ref,
    out_ref, marg_ref,
    e_v, qf, sf, xcat, sb, yr, g, perm1, perm2, swap, back, x_v, ov_g, l_v, p_v, tt, fsc, fs2, o32, obf,
    ovo, cr, cro, xs, xr, pst, zs, zr, ys, yr2, res, mg, st_c, st_x, st_z, st_o,
    esem, ysend, yrecv, zsend, zrecv, xsend, xrecv, csend, crecv,
    vsend, vrecv, wsend, wrecv,
    c2send, c2recv, x2send, x2recv, z2send, z2recv, y2send, y2recv,
    scs, scr, sxs, sxr, szs, szr, ms, mr,
):
    y = lax.axis_index("pos")
    v = lax.axis_index("vocab")
    z = v // NK
    k = lax.rem(v, NK)
    x = k // NC
    c = lax.rem(k, NC)
    line = c * NX + x

    def dev(yy, zz, xx, cc):
        return (yy, zz * NK + xx * NC + cc)

    def xo(o):
        return lax.rem(x + o, NX)

    def ypart(o):
        return dev(lax.rem(y + o, NY), z, x, c)

    def zpart(o):
        return dev(y, lax.rem(z + o, NZ), x, c)

    def xpart(o):
        return dev(y, z, xo(o), c)

    cpart = dev(y, z, x, 1 - c)
    yoffs, zoffs, xoffs = (1, 3, 2), (4, 3, 5, 2, 6, 1, 7), (2, 1, 3)
    pending = []

    def send(src, dst, ss, rs, to):
        cp = pltpu.make_async_remote_copy(
            src_ref=src, dst_ref=dst, send_sem=ss, recv_sem=rs, device_id=to, device_id_type=MESH
        )
        cp.start()
        pending.append(cp)
        return cp

    def rows(start, size):
        return pl.ds(pl.multiple_of(start, 16), size)

    def cols(h):
        return slice(h * DH, (h + 1) * DH)

    barrier = pltpu.get_barrier_semaphore()
    partners = [ypart(o) for o in yoffs] + [zpart(o) for o in zoffs]
    partners += [xpart(o) for o in xoffs] + [cpart]
    for to in partners:
        pl.semaphore_signal(barrier, inc=1, device_id=to, device_id_type=MESH)
    e_copy = pltpu.make_async_copy(e_hbm, e_v, esem)
    e_copy.start()

    for i in range(5):
        qf[2 * i:2 * i + 2] = q_ref[i].astype(F32)
        sf[2 * i:2 * i + 2] = sc_ref[i]
    deq = [qf[:SLOTS, i * 128:(i + 1) * 128] * sf[:SLOTS, i:i + 1] for i in range(D // 128)]
    sq = sum(d * d for d in deq)
    inv = lax.rsqrt(jnp.sum(sq, axis=1, keepdims=True) * (1.0 / D) + 1e-6)
    xcat[...] = jnp.zeros_like(xcat)
    for i in range(D // 128):
        h, rest = divmod(i * 128, DH)
        cc, lane = divmod(rest, CW)
        gn = gain_ref[:, i * 128:(i + 1) * 128]
        xcat[h, cc * SP:cc * SP + SLOTS, lane:lane + 128] = (deq[i] * inv * gn).astype(BF16)

    def bar_len(seq, row):
        n = jnp.zeros(seq.shape, jnp.int32)
        for s in range(8):
            n = jnp.where(seq == s, cnt_ref[s], n)
        return jnp.clip(n - 64 * row, 0, 64)

    def bar_axis(dim):
        b = iota((1, 128) if dim == 1 else (BARS, 1), dim)
        return b, jnp.where(b < BARS, bar_len(jnp.bitwise_and(b, 7), lax.shift_right_logical(b, 3)), 0)

    def rank_of(seq, row, dim):
        b, lb = bar_axis(dim)
        mine, ml = row * 8 + seq, bar_len(seq, row)
        return count((lb > ml) | ((lb == ml) & (b < mine)), dim), ml

    def depth(kk, dim):
        _, lb = bar_axis(dim)
        return lax.shift_right_logical(jnp.maximum(lb - kk, 0) + 7, 3)

    def ahead(zz, nz, dim):
        return jnp.sum(jnp.minimum(zz, nz).astype(F32), axis=dim, keepdims=True).astype(jnp.int32)

    def slot_code(i, dim):
        seq, row = y * 2 + jnp.bitwise_and(i, 1), lax.shift_right_logical(i, 1)
        rank, ml = rank_of(seq, row, dim)
        before = ahead(jnp.full(i.shape, z, jnp.int32), depth(k, dim), dim)
        code = jnp.bitwise_and(rank + before, 3) * 8 + lax.shift_right_logical(rank, 2)
        return jnp.where((v < ml) & (i < SLOTS), code, -1)

    shape = (NY * ROWS, NK * SP)
    i0 = iota((NY * ROWS, 1), 0)
    o_i = div48(i0)
    ci = div6(i0 - o_i * ROWS)
    ri = i0 - o_i * ROWS - ci * CAPR
    want = jnp.bitwise_and(y + o_i, NY - 1) * 8 + ri
    j0 = iota((1, NK * SP), 1)
    cj = lax.shift_right_logical(j0, 4)
    code_j = slot_code(jnp.bitwise_and(j0, SP - 1), 0)
    pick = onehot(
        (jnp.broadcast_to(ci, shape) == jnp.broadcast_to(cj, shape))
        & (jnp.broadcast_to(want, shape) == jnp.broadcast_to(code_j, shape))
    )
    for h in range(H):
        blocks = jnp.dot(pick, xcat[h], preferred_element_type=F32).astype(BF16)
        for o in range(NY):
            sb[h, o] = blocks[o * ROWS:(o + 1) * ROWS]

    pl.semaphore_wait(barrier, len(partners))

    ycp = {}
    for h in range(H):
        for o in yoffs:
            ycp[h, o] = send(sb.at[h, o], yr.at[h, o], ysend.at[h, o], yrecv.at[h, o], ypart(o))

    def place(i, dim):
        zz = div48(i)
        cc = div6(i - zz * ROWS)
        rr = i - zz * ROWS - cc * CAPR
        nz = depth(k, dim)
        before = ahead(zz, nz, dim)
        live = count(nz > zz, dim)
        rank = 4 * rr + jnp.bitwise_and(y - before, 3)
        p = lax.shift_right_logical(before + rank, 2)
        at = jnp.where(p < LR, cc * LR + p, MAIN + cc * OVR + p - LR)
        return jnp.where(rank < live, at, -1)

    perm1[...] = onehot(jnp.broadcast_to(place(iota((1, GR), 1), 0), (M, GR)) == iota((M, GR), 0))

    zcp = {}
    for h in range(H):
        for o in yoffs:
            ycp[h, o].wait_recv()
        own = sb[h, 0].astype(F32)
        for o in yoffs:
            own = own + yr[h, o].astype(F32)
        g[h, rows(z * ROWS, ROWS), :] = own.astype(BF16)
        for o in zoffs:
            mine = g.at[h, rows(z * ROWS, ROWS)]
            zcp[h, o] = send(mine, mine, zsend.at[h, o], zrecv.at[h, o], zpart(o))

    si = iota((128, 1), 0)
    sa, sbb = lax.shift_right_logical(si, 4), jnp.bitwise_and(lax.shift_right_logical(si, 1), 7)
    swap[...] = onehot(
        jnp.broadcast_to(sbb * 16 + sa * 2 + jnp.bitwise_and(si, 1), (128, 128)) == iota((128, 128), 1)
    )
    perm2[...] = onehot(
        jnp.broadcast_to(place(iota((GR, 1), 0), 1), (GR, M)) == iota((GR, M), 1)
    )
    shape = (NK * SP, NY * ROWS)
    j0 = iota((1, NY * ROWS), 1)
    o_j = div48(j0)
    cj = div6(j0 - o_j * ROWS)
    rj = j0 - o_j * ROWS - cj * CAPR
    have = jnp.bitwise_and(y + NY - o_j, NY - 1) * 8 + rj
    i0 = iota((NK * SP, 1), 0)
    ci = lax.shift_right_logical(i0, 4)
    code_i = slot_code(jnp.bitwise_and(i0, SP - 1), 1)
    back[...] = onehot(
        (jnp.broadcast_to(ci, shape) == jnp.broadcast_to(cj, shape))
        & (jnp.broadcast_to(code_i, shape) == jnp.broadcast_to(have, shape))
    )

    xcp, ccp, vcp, wcp = {}, {}, {}, {}

    def main_at(ln, h):
        return x_v.at[rows(ln * LR, LR), pl.ds(h * DH, DH)]

    def further_at(ln, h):
        return ov_g.at[h, rows(ln * OV, OV)]

    def x_send(ln, h, o, to):
        a, b = main_at(ln, h), further_at(ln, h)
        xcp[h, o] = send(a, a, xsend.at[h, o], xrecv.at[h, o], to)
        vcp[h, o] = send(b, b, vsend.at[h, o], vrecv.at[h, o], to)

    def c_send(ln, h, o):
        a, b = main_at(ln, h), further_at(ln, h)
        ccp[h, o] = send(a, a, csend.at[h, o], crecv.at[h, o], cpart)
        wcp[h, o] = send(b, b, wsend.at[h, o], wrecv.at[h, o], cpart)

    for h in range(H):
        for o in zoffs:
            zcp[h, o].wait_recv()
        lines = jnp.dot(perm1[...], g[h], preferred_element_type=F32).astype(BF16)
        for cc in range(NK):
            ln = slice(h * DH + cc * CW, h * DH + (cc + 1) * CW)
            x_v[rows(line * LR, LR), ln] = lines[cc * LR:(cc + 1) * LR]
        ov_g[h, rows(line * OV, OV)] = lines[MAIN:]
        x_send(line, h, 1, xpart(1))
        x_send(line, h, 3, xpart(3))
        c_send(line, h, 0)

    def x_got(h, o):
        xcp[h, o].wait_recv()
        vcp[h, o].wait_recv()

    for h, o in ((0, 1), (1, 3)):
        x_got(h, o)
        ln = c * NX + xo(NX - o)
        x_send(ln, h, 2, xpart(o))
        c_send(ln, h, o)
        other = NX - o
        x_got(h, other)
        c_send(c * NX + xo(NX - other), h, other)

    for h in range(H):
        x_got(h, 2)
        c_send(c * NX + xo(2), h, 2)
        for o in (0, 1, 3, 2):
            ccp[h, o].wait_recv()
            wcp[h, o].wait_recv()
        further = jnp.dot(swap[...], ov_g[h], preferred_element_type=F32).astype(BF16)
        for cc in range(NK):
            x_v[MAIN:, h * DH + cc * CW:h * DH + (cc + 1) * CW] = further[cc * OV:(cc + 1) * OV]
        if h == 0:
            e_copy.wait()

        def mm1(i, carry):
            n = pl.ds(pl.multiple_of(i * 256, 256), 256)
            part = lax.dot_general(
                x_v[:, cols(h)], e_v[n, cols(h)],
                (((1,), (1,)), ((), ())), preferred_element_type=F32,
            )
            l_v[:, n] = part if h == 0 else l_v[:, n] + part
            return carry

        lax.fori_loop(0, V // 256, mm1, 0)

    for start, size in ((0, 128), (128, 128), (MAIN, OV)):
        r = slice(start, start + size)
        t1 = l_v[r, 0:128]
        t2 = jnp.full((size, 128), -jnp.inf, F32)
        for j in range(1, V // 128):
            val = l_v[r, j * 128:(j + 1) * 128]
            t2 = jnp.maximum(t2, jnp.minimum(t1, val))
            t1 = jnp.maximum(t1, val)
        top = jnp.max(t1, axis=1, keepdims=True)
        acc = jnp.zeros((size, 128), F32)
        for j in range(V // 128):
            e = jnp.exp(l_v[r, j * 128:(j + 1) * 128] - top)
            acc = acc + e
            p_v[r, j * 128:(j + 1) * 128] = e.astype(BF16)
        if size < 128:
            pad = jnp.ones((128 - size, 128), F32)
            t1, t2, acc = (jnp.concatenate([a, pad], axis=0) for a in (t1, t2, acc))
        for n, a in enumerate((t1, t2, acc)):
            tt[n, :, start:start + 128] = a.T
    m1, m2, sm = tt[0], tt[1], tt[2]
    n = 128
    while n > 1:
        n //= 2
        a1, b1 = m1[:n], m1[n:]
        m2 = jnp.maximum(jnp.minimum(a1, b1), jnp.maximum(m2[:n], m2[n:]))
        m1 = jnp.maximum(a1, b1)
        sm = sm[:n] + sm[n:]
    loc = m1

    def put(slot, parts):
        for n in range(3):
            st_o[slot, n:n + 1] = parts[n]

    def got3(ref):
        return (ref[0:1], ref[1:2], ref[2:3])

    def spread(ref, factor):
        for i in range(0, ML, 128):
            size = min(128, M - i)
            ref[i:i + size] = jnp.broadcast_to(factor[:, i:i + 128], (128, 128)).T[:size]

    def mm2(lo, hi):
        def body(i, carry):
            n = pl.ds(pl.multiple_of(i * 256, 256), 256)
            o32[:, n] = jnp.dot(p_v[...], e_v[:, n], preferred_element_type=F32)
            return carry

        lax.fori_loop(lo, hi, body, 0)

    quarter = DH // 512
    st_o[...] = jnp.zeros_like(st_o)
    cur = (m1, m2, sm)
    put(0, cur)
    cp = send(st_o.at[0], st_c, scs, scr, cpart)
    mm2(0, quarter)
    cp.wait_recv()
    cur = merge([cur, got3(st_c)])
    put(1, cur)
    cps = [send(st_o.at[1], st_x.at[o], sxs.at[o], sxr.at[o], xpart(o)) for o in xoffs]
    mm2(quarter, 2 * quarter)
    for cp in cps:
        cp.wait_recv()
    cur = merge([cur] + [got3(st_x[o]) for o in xoffs])
    put(2, cur)
    scp = [send(st_o.at[2], st_z.at[o], szs.at[o], szr.at[o], zpart(o)) for o in zoffs]
    spread(fsc, jnp.exp(loc - cur[0]))

    c2, x2, z2, y2 = {}, {}, {}, {}

    def scaled(i, carry):
        n = pl.ds(pl.multiple_of(i * 128, 128), 128)
        obf[:, n] = (o32[:, n] * fsc[...]).astype(BF16)
        return carry

    def mm2_scaled(i, carry):
        n = pl.ds(pl.multiple_of(i * 256, 256), 256)
        part = jnp.dot(p_v[...], e_v[:, n], preferred_element_type=F32)
        for t in range(2):
            at = pl.ds(pl.multiple_of(i * 256 + t * 128, 128), 128)
            obf[:, at] = (part[:, t * 128:(t + 1) * 128] * fsc[...]).astype(BF16)
        return carry

    def core_send(h):
        src = obf.at[rows((1 - c) * NX * LR, NX * LR), pl.ds(h * DH, DH)]
        c2[h, 0] = send(src, cr.at[h], c2send.at[h, 0], c2recv.at[h, 0], cpart)
        stack = jnp.concatenate(
            [obf[MAIN:, h * DH + cc * CW:h * DH + (cc + 1) * CW] for cc in range(NK)], axis=0
        )
        ovo[h] = jnp.dot(swap[...], stack, preferred_element_type=F32).astype(BF16)
        src = ovo.at[h, rows((1 - c) * NX * OV, NX * OV)]
        c2[h, 1] = send(src, cro.at[h], c2send.at[h, 1], c2recv.at[h, 1], cpart)

    lax.fori_loop(0, DH // 128, scaled, 0)
    core_send(0)
    lax.fori_loop(DH // 256, D // 256, mm2_scaled, 0)
    core_send(1)

    def x2_send(h, o, to):
        x2[h, o] = send(xs.at[h, o], xr.at[h, o], x2send.at[h, o], x2recv.at[h, o], xpart(to))

    def chip_sum(h, o):
        xx = xo(o)
        at = rows((c * NX + xx) * LR, LR)
        for cc in range(NK):
            mine = obf[at, h * DH + cc * CW:h * DH + (cc + 1) * CW].astype(F32)
            theirs = cr[h, rows(xx * LR, LR), cc * CW:(cc + 1) * CW].astype(F32)
            xs[h, o, cc * LR:(cc + 1) * LR] = (mine + theirs).astype(BF16)
        mine = ovo[h, rows((c * NX + xx) * OV, OV)].astype(F32)
        theirs = cro[h, rows(xx * OV, OV)].astype(F32)
        xs[h, o, MAIN:] = (mine + theirs).astype(BF16)

    for h, o in ((0, 1), (1, 3)):
        c2[h, 0].wait_recv()
        c2[h, 1].wait_recv()
        chip_sum(h, 2)
        x2_send(h, 2, o)
        chip_sum(h, NX - o)
        x2_send(h, NX - o, NX - o)
        chip_sum(h, o)
        chip_sum(h, 0)
    for h, o in ((0, 1), (1, 3)):
        x2[h, 2].wait_recv()
        xs[h, o] = (xs[h, o].astype(F32) + xr[h, 2].astype(F32)).astype(BF16)
        x2_send(h, o, o)

    for cp in scp:
        cp.wait_recv()
    m8 = cur[0]
    m1, m2, sm = merge([cur] + [got3(st_z[o]) for o in zoffs])
    spread(fs2, jnp.exp(m8 - m1) / sm * 64.0)
    margin = (1.0 - jnp.exp(m2 - m1)) / sm
    mg[y] = jnp.broadcast_to(margin, (8, ML))
    mcp = [send(mg.at[y], mg.at[y], ms.at[o], mr.at[o], ypart(o)) for o in yoffs]

    f_main = fs2[rows(line * LR, LR)]
    f_a = fs2[pl.ds(MAIN + line * OVR, 1)]
    f_b = fs2[pl.ds(MAIN + line * OVR + 1, 1)]
    f_ov = jnp.where(jnp.bitwise_and(iota((OV, 128), 0), 1) == 0, f_a, f_b)

    for h in range(H):
        for o in (1, 3):
            x2[h, o].wait_recv()
        for lane in range(0, CW, 128):
            ln = slice(lane, lane + 128)
            for cc in range(NK + 1):
                r = slice(cc * LR, min(cc * LR + LR, M))
                tot = xs[h, 0, r, ln].astype(F32) + xr[h, 1, r, ln].astype(F32)
                tot = tot + xr[h, 3, r, ln].astype(F32)
                pst[r, ln] = (tot * (f_main if cc < NK else f_ov)).astype(BF16)
        zs[h] = jnp.dot(perm2[...], pst[...], preferred_element_type=F32).astype(BF16)
        for o in zoffs:
            src = zs.at[h, rows(lax.rem(z + o, NZ) * ROWS, ROWS)]
            z2[h, o] = send(src, zr.at[h, o], z2send.at[h, o], z2recv.at[h, o], zpart(o))

    for cp in mcp:
        cp.wait_recv()
    lane = iota((1, ML), 1)
    lm = jnp.minimum(lane, M - 1)
    ln = jnp.where(lm < MAIN, lax.shift_right_logical(lm, 5), lax.shift_right_logical(lm - MAIN, 1))
    p = jnp.where(lm < MAIN, jnp.bitwise_and(lm, LR - 1), LR + jnp.bitwise_and(lm, 1))
    kk = jnp.bitwise_and(ln, NX - 1) * NC + lax.shift_right_logical(ln, 2)
    nz = depth(kk, 0)
    befores = [ahead(jnp.full((1, ML), n, jnp.int32), nz, 0) for n in range(NZ + 1)]
    slot = iota((SP, 1), 0)
    rank_i, len_i = rank_of(y * 2 + jnp.bitwise_and(slot, 1), lax.shift_right_logical(slot, 1), 1)
    by_col = jnp.zeros((SP, 64), F32)
    for yy in range(NY):
        gi = 4 * p + yy
        zz = jnp.zeros((1, ML), jnp.int32)
        first = jnp.zeros((1, ML), jnp.int32)
        for n in range(1, NZ):
            past = befores[n] <= gi
            zz = jnp.where(past, n, zz)
            first = jnp.where(past, befores[n], first)
        rank = jnp.where((gi < befores[NZ]) & (lane < M), gi - first, -1)
        vals = jnp.where(
            jnp.broadcast_to(rank, (SP, ML)) == jnp.broadcast_to(rank_i, (SP, ML)),
            jnp.broadcast_to(mg[yy, 0:1], (SP, ML)), 0.0,
        )
        hit = jnp.broadcast_to(zz * NK + kk, (64, ML)) == iota((64, ML), 0)
        by_col = by_col + lax.dot_general(
            vals, jnp.where(hit, 1.0, 0.0), (((1,), (1,)), ((), ())),
            preferred_element_type=F32, precision=lax.Precision.HIGHEST,
        )
    masked = (iota((SP, 64), 1) < len_i) & (iota((SP, 64), 0) < SLOTS)
    by_col = jnp.where(masked, by_col, 0.0)
    wide = (2, 128)
    marg = jnp.zeros(wide, F32)
    for t in range(LEN_DEV):
        target = v * LEN_DEV + t
        for s2 in range(2):
            hit = sum(
                jnp.where(pos_ref[r5, s2:s2 + 1] == target, by_col[2 * r5 + s2:2 * r5 + s2 + 1], 0.0)
                for r5 in range(5)
            )
            val = jnp.broadcast_to(jnp.sum(hit, axis=1, keepdims=True), wide)
            marg = jnp.where((iota(wide, 1) == t) & (iota(wide, 0) == s2), val, marg)
    marg_ref[...] = marg[:, :LEN_DEV]

    for h in range(H):
        for o in zoffs:
            z2[h, o].wait_recv()
        tot = zs[h, rows(z * ROWS, ROWS), :].astype(F32)
        for o in zoffs:
            tot = tot + zr[h, o].astype(F32)
        ys[h] = tot.astype(BF16)
        yr2[h, 0] = ys[h]
        for o in yoffs:
            y2[h, o] = send(ys.at[h], yr2.at[h, o], y2send.at[h, o], y2recv.at[h, o], ypart(o))

    for h in range(H):
        for o in yoffs:
            y2[h, o].wait_recv()
        cat = jnp.concatenate([yr2[h, o] for o in range(NY)], axis=0)
        got = jnp.dot(back[...], cat, preferred_element_type=F32)
        for cc in range(NK):
            res[:, h * DH + cc * CW:h * DH + (cc + 1) * CW] = got[cc * SP:(cc + 1) * SP]
    for i in range(5):
        out_ref[i] = res[2 * i:2 * i + 2].astype(BF16)
    for cp in pending:
        cp.wait_send()


def readout(q, sc, gain, table, counts, positions):
    dma = pltpu.SemaphoreType.DMA
    vm = pl.BlockSpec(memory_space=pltpu.VMEM)
    return pl.pallas_call(
        kernel,
        out_shape=(
            jax.ShapeDtypeStruct(q.shape, BF16),
            jax.ShapeDtypeStruct((2, LEN_DEV), F32),
        ),
        in_specs=[
            vm, vm, vm, pl.BlockSpec(memory_space=pl.ANY), pl.BlockSpec(memory_space=pltpu.SMEM), vm
        ],
        out_specs=(vm, vm),
        scratch_shapes=[
            pltpu.VMEM((V, D), BF16),
            pltpu.VMEM((SP, D), F32),
            pltpu.VMEM((SP, D // 128), F32),
            pltpu.VMEM((H, NK * SP, CW), BF16),
            pltpu.VMEM((H, NY, ROWS, CW), BF16),
            pltpu.VMEM((H, NY, ROWS, CW), BF16),
            pltpu.VMEM((H, GR, CW), BF16),
            pltpu.VMEM((M, GR), BF16),
            pltpu.VMEM((GR, M), BF16),
            pltpu.VMEM((128, 128), BF16),
            pltpu.VMEM((NK * SP, NY * ROWS), BF16),
            pltpu.VMEM((M, D), BF16),
            pltpu.VMEM((H, NK * OV, CW), BF16),
            pltpu.VMEM((M, V), F32),
            pltpu.VMEM((M, V), BF16),
            pltpu.VMEM((3, 128, ML), F32),
            pltpu.VMEM((M, 128), F32),
            pltpu.VMEM((M, 128), F32),
            pltpu.VMEM((M, DH), F32),
            pltpu.VMEM((M, D), BF16),
            pltpu.VMEM((H, NK * OV, CW), BF16),
            pltpu.VMEM((H, NX * LR, DH), BF16),
            pltpu.VMEM((H, NX * OV, CW), BF16),
            pltpu.VMEM((H, NX, M, CW), BF16),
            pltpu.VMEM((H, NX, M, CW), BF16),
            pltpu.VMEM((M, CW), BF16),
            pltpu.VMEM((H, GR, CW), BF16),
            pltpu.VMEM((H, NZ, ROWS, CW), BF16),
            pltpu.VMEM((H, ROWS, CW), BF16),
            pltpu.VMEM((H, NY, ROWS, CW), BF16),
            pltpu.VMEM((SP, D), F32),
            pltpu.VMEM((NY, 8, ML), F32),
            pltpu.VMEM((8, ML), F32),
            pltpu.VMEM((NX, 8, ML), F32),
            pltpu.VMEM((NZ, 8, ML), F32),
            pltpu.VMEM((3, 8, ML), F32),
            dma,
            dma((H, NY)), dma((H, NY)), dma((H, NZ)), dma((H, NZ)),
            dma((H, NX)), dma((H, NX)), dma((H, NX)), dma((H, NX)),
            dma((H, NX)), dma((H, NX)), dma((H, NX)), dma((H, NX)),
            dma((H, 2)), dma((H, 2)), dma((H, NX)), dma((H, NX)),
            dma((H, NZ)), dma((H, NZ)), dma((H, NY)), dma((H, NY)),
            dma, dma, dma((NX,)), dma((NX,)), dma((NZ,)), dma((NZ,)), dma((NY,)), dma((NY,)),
        ],
        compiler_params=pltpu.CompilerParams(
            collective_id=0, has_side_effects=True, vmem_limit_bytes=60 << 20
        ),
        cost_estimate=pl.CostEstimate(
            flops=4 * M * V * D, bytes_accessed=2 * V * D, transcendentals=M * V
        ),
        name="readout",
    )(q, sc, gain, table, counts, positions)


def on_device(quantized, scales, norm_gain, embed_table, counts, positions):
    expected, margins = readout(
        quantized[0], scales[0], norm_gain.reshape(1, D), embed_table, counts,
        positions.transpose(1, 2, 0),
    )
    return (expected[None], margins)


def solution(mesh):
    in_specs = (
        P("vocab", None, "pos", None),
        P("vocab", None, "pos", None),
        P(),
        P("vocab", None),
        P(),
        P(None, None, "pos"),
    )
    out_specs = (P("vocab", None, "pos", None), P("pos", "vocab"))
    return jax.shard_map(
        on_device, mesh=mesh, in_specs=in_specs, out_specs=out_specs, check_vma=False
    )
```

time: 96.5 us -> 80.6 us (0.84)
  Pallas kernels: 87.4 us -> 77 us
  local copies, waits for them, and re-layouts: 7.31 us -> 2.81 us
    pallas_call x1, Pallas kernels: 87.4 us -> 77 us  [readout(): pl.pallas_call(kernel, out_shape=(jax.ShapeDtypeStruct(q.shape, BF16), ja...]
    reshape x4 -> x0, local copies, waits for them, and re-layouts: 4.57 us -> none  [the longest x1 1.61 us: on_device(): expected = out[:SLOTS].reshape(1, rows, seqs, D)]
    unnamed x5 -> x2, local copies, waits for them, and re-layouts: 0.66 us -> 2.81 us
where the time goes in v2:
time: 80.6 us; the launch traced here: 80.5 us
  Pallas kernels  77 us (96%)
  local copies, waits for them, and re-layouts  2.81 us (3%)
    pallas_call x1, Pallas kernels, readout(): pl.pallas_call(kernel, out_shape=(jax.ShapeDtypeStruct(q.shape, BF16), ja...  77 us
    unnamed x2, local copies, waits for them, and re-layouts  2.81 us

profile of v2, /device:TPU:16, one launch (start us, length us, event | category | flops | bytes accessed | tf_op | source)
XLA Modules:
  0.0 80.5 jit_solution(13243675373493757210)
XLA Ops:
  0.6 77.0 %readout.1 = (bf16[5,2,4096]{2,1,0:T(2,128)(2,1)}, f32[2,10]{1,0:T(2,128)}) custom-call(bf16[5,2,4096]{2,1,0:T(2,128)(2,1)} %bitcast.6, f32[5,2,32]{2,1,0:T(2,128)} %bitcast.8, f32[1,4096]{1,0:T(1,128)} %bitcast.7, bf16[1280,4096]{1,0:T(8,128)(2,1)} %e_hbm.1, s32[8]{0:T(128)} %cnt_ref.1, s32[5,2,64]{2,1,0:T(2,128)} %bitcast.9), custom_call_target="tpu_custom_call" | custom-call | flops 5704253440 | bytes 10485760 | tf_op jit(solution)/shard_map/readout/pallas_call | solution.py:532
  77.7 1.6 %copy.10 = bf16[1,5,2,4096]{3,2,1,0:T(2,128)(2,1)} copy(bf16[1,5,2,4096]{3,2,1,0:T(2,128)(2,1)} %bitcast.5) | data formatting | bytes 163840
  79.2 1.2 %copy.11 = f32[2,10]{1,0:T(2,128)} copy(f32[2,10]{1,0:T(2,128)} %get-tuple-element.9) | data formatting | bytes 160

commit v3 on v2

--- a/solution.py
+++ b/solution.py
@@ -66,7 +66,7 @@
 def kernel(
     q_ref, sc_ref, gain_ref, e_hbm, cnt_ref, pos_ref,
     out_ref, marg_ref,
-    e_v, qf, sf, xcat, sb, yr, g, perm1, perm2, swap, back, x_v, ov_g, l_v, p_v, tt, fsc, fs2, o32, obf,
+    e_v, qf, sf, xcat, sb, yr, g, perm1, perm2, swap, back, x_v, ov_g, l_v, p_v, tt, fsc, fs2, obf,
     ovo, cr, cro, xs, xr, pst, zs, zr, ys, yr2, res, mg, st_c, st_x, st_z, st_o,
     esem, ysend, yrecv, zsend, zrecv, xsend, xrecv, csend, crecv,
     vsend, vrecv, wsend, wrecv,
@@ -263,26 +263,15 @@
             ln = slice(h * DH + cc * CW, h * DH + (cc + 1) * CW)
             x_v[rows(line * LR, LR), ln] = lines[cc * LR:(cc + 1) * LR]
         ov_g[h, rows(line * OV, OV)] = lines[MAIN:]
-        x_send(line, h, 1, xpart(1))
-        x_send(line, h, 3, xpart(3))
+        for o in xoffs:
+            x_send(line, h, o, xpart(o))
         c_send(line, h, 0)
 
-    def x_got(h, o):
-        xcp[h, o].wait_recv()
-        vcp[h, o].wait_recv()
-
-    for h, o in ((0, 1), (1, 3)):
-        x_got(h, o)
-        ln = c * NX + xo(NX - o)
-        x_send(ln, h, 2, xpart(o))
-        c_send(ln, h, o)
-        other = NX - o
-        x_got(h, other)
-        c_send(c * NX + xo(NX - other), h, other)
-
-    for h in range(H):
-        x_got(h, 2)
-        c_send(c * NX + xo(2), h, 2)
+    for h in range(H):
+        for o in (1, 3, 2):
+            xcp[h, o].wait_recv()
+            vcp[h, o].wait_recv()
+            c_send(c * NX + xo(NX - o), h, o)
         for o in (0, 1, 3, 2):
             ccp[h, o].wait_recv()
             wcp[h, o].wait_recv()
@@ -293,7 +282,7 @@
             e_copy.wait()
 
         def mm1(i, carry):
-            n = pl.ds(pl.multiple_of(i * 256, 256), 256)
+            n = pl.ds(pl.multiple_of(i * 640, 640), 640)
             part = lax.dot_general(
                 x_v[:, cols(h)], e_v[n, cols(h)],
                 (((1,), (1,)), ((), ())), preferred_element_type=F32,
@@ -301,7 +290,7 @@
             l_v[:, n] = part if h == 0 else l_v[:, n] + part
             return carry
 
-        lax.fori_loop(0, V // 256, mm1, 0)
+        lax.fori_loop(0, V // 640, mm1, 0)
 
     for start, size in ((0, 128), (128, 128), (MAIN, OV)):
         r = slice(start, start + size)
@@ -344,46 +333,11 @@
             size = min(128, M - i)
             ref[i:i + size] = jnp.broadcast_to(factor[:, i:i + 128], (128, 128)).T[:size]
 
-    def mm2(lo, hi):
-        def body(i, carry):
-            n = pl.ds(pl.multiple_of(i * 256, 256), 256)
-            o32[:, n] = jnp.dot(p_v[...], e_v[:, n], preferred_element_type=F32)
-            return carry
-
-        lax.fori_loop(lo, hi, body, 0)
-
-    quarter = DH // 512
-    st_o[...] = jnp.zeros_like(st_o)
-    cur = (m1, m2, sm)
-    put(0, cur)
-    cp = send(st_o.at[0], st_c, scs, scr, cpart)
-    mm2(0, quarter)
-    cp.wait_recv()
-    cur = merge([cur, got3(st_c)])
-    put(1, cur)
-    cps = [send(st_o.at[1], st_x.at[o], sxs.at[o], sxr.at[o], xpart(o)) for o in xoffs]
-    mm2(quarter, 2 * quarter)
-    for cp in cps:
-        cp.wait_recv()
-    cur = merge([cur] + [got3(st_x[o]) for o in xoffs])
-    put(2, cur)
-    scp = [send(st_o.at[2], st_z.at[o], szs.at[o], szr.at[o], zpart(o)) for o in zoffs]
-    spread(fsc, jnp.exp(loc - cur[0]))
-
     c2, x2, z2, y2 = {}, {}, {}, {}
 
-    def scaled(i, carry):
-        n = pl.ds(pl.multiple_of(i * 128, 128), 128)
-        obf[:, n] = (o32[:, n] * fsc[...]).astype(BF16)
-        return carry
-
-    def mm2_scaled(i, carry):
-        n = pl.ds(pl.multiple_of(i * 256, 256), 256)
-        part = jnp.dot(p_v[...], e_v[:, n], preferred_element_type=F32)
-        for t in range(2):
-            at = pl.ds(pl.multiple_of(i * 256 + t * 128, 128), 128)
-            obf[:, at] = (part[:, t * 128:(t + 1) * 128] * fsc[...]).astype(BF16)
-        return carry
+    def mm2(i):
+        n = slice(i * 1024, (i + 1) * 1024)
+        obf[:, n] = jnp.dot(p_v[...], e_v[:, n], preferred_element_type=F32).astype(BF16)
 
     def core_send(h):
         src = obf.at[rows((1 - c) * NX * LR, NX * LR), pl.ds(h * DH, DH)]
@@ -395,62 +349,81 @@
         src = ovo.at[h, rows((1 - c) * NX * OV, NX * OV)]
         c2[h, 1] = send(src, cro.at[h], c2send.at[h, 1], c2recv.at[h, 1], cpart)
 
-    lax.fori_loop(0, DH // 128, scaled, 0)
+    st_o[...] = jnp.zeros_like(st_o)
+    cur = (m1, m2, sm)
+    put(0, cur)
+    cp = send(st_o.at[0], st_c, scs, scr, cpart)
+    mm2(0)
+    cp.wait_recv()
+    loc2 = st_c[0:1]
+    cur = merge([cur, got3(st_c)])
+    put(1, cur)
+    cps = [send(st_o.at[1], st_x.at[o], sxs.at[o], sxr.at[o], xpart(o)) for o in xoffs]
+    mm2(1)
     core_send(0)
-    lax.fori_loop(DH // 256, D // 256, mm2_scaled, 0)
+    mm2(2)
+    for cp in cps:
+        cp.wait_recv()
+    cur = merge([cur] + [got3(st_x[o]) for o in xoffs])
+    put(2, cur)
+    scp = [send(st_o.at[2], st_z.at[o], szs.at[o], szr.at[o], zpart(o)) for o in zoffs]
+    spread(fsc, jnp.exp(loc - cur[0]))
+    spread(fs2, jnp.exp(loc2 - cur[0]))
+    mm2(3)
     core_send(1)
 
     def x2_send(h, o, to):
         x2[h, o] = send(xs.at[h, o], xr.at[h, o], x2send.at[h, o], x2recv.at[h, o], xpart(to))
 
+    def further_factor(ref, ln):
+        pair = [ref[pl.ds(MAIN + ln * OVR + e, 1)] for e in range(OVR)]
+        return jnp.where(jnp.bitwise_and(iota((OV, 128), 0), 1) == 0, pair[0], pair[1])
+
     def chip_sum(h, o):
         xx = xo(o)
-        at = rows((c * NX + xx) * LR, LR)
-        for cc in range(NK):
-            mine = obf[at, h * DH + cc * CW:h * DH + (cc + 1) * CW].astype(F32)
-            theirs = cr[h, rows(xx * LR, LR), cc * CW:(cc + 1) * CW].astype(F32)
-            xs[h, o, cc * LR:(cc + 1) * LR] = (mine + theirs).astype(BF16)
-        mine = ovo[h, rows((c * NX + xx) * OV, OV)].astype(F32)
-        theirs = cro[h, rows(xx * OV, OV)].astype(F32)
-        xs[h, o, MAIN:] = (mine + theirs).astype(BF16)
-
-    for h, o in ((0, 1), (1, 3)):
+        ln = c * NX + xx
+        at = rows(ln * LR, LR)
+        fa, fb = fsc[at], fs2[at]
+        for lane in range(0, DH, 128):
+            mine = obf[at, h * DH + lane:h * DH + lane + 128].astype(F32)
+            theirs = cr[h, rows(xx * LR, LR), lane:lane + 128].astype(F32)
+            cc, sub = divmod(lane, CW)
+            xs[h, o, cc * LR:(cc + 1) * LR, sub:sub + 128] = (mine * fa + theirs * fb).astype(BF16)
+        fa, fb = further_factor(fsc, ln), further_factor(fs2, ln)
+        for sub in range(0, CW, 128):
+            mine = ovo[h, rows(ln * OV, OV), sub:sub + 128].astype(F32)
+            theirs = cro[h, rows(xx * OV, OV), sub:sub + 128].astype(F32)
+            xs[h, o, MAIN:, sub:sub + 128] = (mine * fa + theirs * fb).astype(BF16)
+
+    for h in range(H):
         c2[h, 0].wait_recv()
         c2[h, 1].wait_recv()
-        chip_sum(h, 2)
-        x2_send(h, 2, o)
-        chip_sum(h, NX - o)
-        x2_send(h, NX - o, NX - o)
-        chip_sum(h, o)
-        chip_sum(h, 0)
-    for h, o in ((0, 1), (1, 3)):
-        x2[h, 2].wait_recv()
-        xs[h, o] = (xs[h, o].astype(F32) + xr[h, 2].astype(F32)).astype(BF16)
-        x2_send(h, o, o)
+        for o in (2, 1, 3, 0):
+            chip_sum(h, o)
+            if o:
+                x2_send(h, o, o)
 
     for cp in scp:
         cp.wait_recv()
     m8 = cur[0]
     m1, m2, sm = merge([cur] + [got3(st_z[o]) for o in zoffs])
-    spread(fs2, jnp.exp(m8 - m1) / sm * 64.0)
+    spread(fsc, jnp.exp(m8 - m1) / sm * 64.0)
     margin = (1.0 - jnp.exp(m2 - m1)) / sm
     mg[y] = jnp.broadcast_to(margin, (8, ML))
     mcp = [send(mg.at[y], mg.at[y], ms.at[o], mr.at[o], ypart(o)) for o in yoffs]
 
-    f_main = fs2[rows(line * LR, LR)]
-    f_a = fs2[pl.ds(MAIN + line * OVR, 1)]
-    f_b = fs2[pl.ds(MAIN + line * OVR + 1, 1)]
-    f_ov = jnp.where(jnp.bitwise_and(iota((OV, 128), 0), 1) == 0, f_a, f_b)
-
-    for h in range(H):
-        for o in (1, 3):
+    f_main = fsc[rows(line * LR, LR)]
+    f_ov = further_factor(fsc, line)
+
+    for h in range(H):
+        for o in (1, 3, 2):
             x2[h, o].wait_recv()
         for lane in range(0, CW, 128):
             ln = slice(lane, lane + 128)
             for cc in range(NK + 1):
                 r = slice(cc * LR, min(cc * LR + LR, M))
                 tot = xs[h, 0, r, ln].astype(F32) + xr[h, 1, r, ln].astype(F32)
-                tot = tot + xr[h, 3, r, ln].astype(F32)
+                tot = tot + xr[h, 3, r, ln].astype(F32) + xr[h, 2, r, ln].astype(F32)
                 pst[r, ln] = (tot * (f_main if cc < NK else f_ov)).astype(BF16)
         zs[h] = jnp.dot(perm2[...], pst[...], preferred_element_type=F32).astype(BF16)
         for o in zoffs:
@@ -558,7 +531,6 @@
             pltpu.VMEM((3, 128, ML), F32),
             pltpu.VMEM((M, 128), F32),
             pltpu.VMEM((M, 128), F32),
-            pltpu.VMEM((M, DH), F32),
             pltpu.VMEM((M, D), BF16),
             pltpu.VMEM((H, NK * OV, CW), BF16),
             pltpu.VMEM((H, NX * LR, DH), BF16),

time: 80.6 us -> 75.3 us (0.934)
  Pallas kernels: 77 us -> 71 us
    pallas_call x1, Pallas kernels: 77 us -> 71 us  [readout(): pl.pallas_call(kernel, out_shape=(jax.ShapeDtypeStruct(q.shape, BF16), ja...]
where the time goes in v3:
time: 75.3 us; the launch traced here: 74.5 us
  Pallas kernels  71 us (94%)
  local copies, waits for them, and re-layouts  2.81 us (4%)
    pallas_call x1, Pallas kernels, readout(): pl.pallas_call(kernel, out_shape=(jax.ShapeDtypeStruct(q.shape, BF16), ja...  71 us
    unnamed x2, local copies, waits for them, and re-layouts  2.81 us

profile of v3, /device:TPU:16, one launch (start us, length us, event | category | flops | bytes accessed | tf_op | source)
XLA Modules:
  0.0 74.5 jit_solution(3558001594364539466)
XLA Ops:
  0.6 71.0 %readout.1 = (bf16[5,2,4096]{2,1,0:T(2,128)(2,1)}, f32[2,10]{1,0:T(2,128)}) custom-call(bf16[5,2,4096]{2,1,0:T(2,128)(2,1)} %bitcast.6, f32[5,2,32]{2,1,0:T(2,128)} %bitcast.8, f32[1,4096]{1,0:T(1,128)} %bitcast.7, bf16[1280,4096]{1,0:T(8,128)(2,1)} %e_hbm.1, s32[8]{0:T(128)} %cnt_ref.1, s32[5,2,64]{2,1,0:T(2,128)} %bitcast.9), custom_call_target="tpu_custom_call" | custom-call | flops 5704253440 | bytes 10485760 | tf_op jit(solution)/shard_map/readout/pallas_call | solution.py:505
  71.6 1.6 %copy.10 = bf16[1,5,2,4096]{3,2,1,0:T(2,128)(2,1)} copy(bf16[1,5,2,4096]{3,2,1,0:T(2,128)(2,1)} %bitcast.5) | data formatting | bytes 163840
  73.2 1.2 %copy.11 = f32[2,10]{1,0:T(2,128)} copy(f32[2,10]{1,0:T(2,128)} %get-tuple-element.9) | data formatting | bytes 160

commit v4 on v3

--- a/solution.py
+++ b/solution.py
@@ -25,7 +25,7 @@
 M = MAIN + OV
 ML = 384
 V = 1280
-H = 2
+H = 4
 DH = D // H
 CW = DH // NK
 SLOTS = 10
@@ -66,7 +66,7 @@
 def kernel(
     q_ref, sc_ref, gain_ref, e_hbm, cnt_ref, pos_ref,
     out_ref, marg_ref,
-    e_v, qf, sf, xcat, sb, yr, g, perm1, perm2, swap, back, x_v, ov_g, l_v, p_v, tt, fsc, fs2, obf,
+    e_v, qf, sf, xcat, sb, yr, g, perm1, perm2, swap, back, x_v, ov_g, l_v, p_v, tt, fsc, fs2, fx, obf,
     ovo, cr, cro, xs, xr, pst, zs, zr, ys, yr2, res, mg, st_c, st_x, st_z, st_o,
     esem, ysend, yrecv, zsend, zrecv, xsend, xrecv, csend, crecv,
     vsend, vrecv, wsend, wrecv,
@@ -267,11 +267,7 @@
             x_send(line, h, o, xpart(o))
         c_send(line, h, 0)
 
-    for h in range(H):
-        for o in (1, 3, 2):
-            xcp[h, o].wait_recv()
-            vcp[h, o].wait_recv()
-            c_send(c * NX + xo(NX - o), h, o)
+    def mm1(h):
         for o in (0, 1, 3, 2):
             ccp[h, o].wait_recv()
             wcp[h, o].wait_recv()
@@ -281,7 +277,7 @@
         if h == 0:
             e_copy.wait()
 
-        def mm1(i, carry):
+        def body(i, carry):
             n = pl.ds(pl.multiple_of(i * 640, 640), 640)
             part = lax.dot_general(
                 x_v[:, cols(h)], e_v[n, cols(h)],
@@ -290,7 +286,16 @@
             l_v[:, n] = part if h == 0 else l_v[:, n] + part
             return carry
 
-        lax.fori_loop(0, V // 640, mm1, 0)
+        lax.fori_loop(0, V // 640, body, 0)
+
+    for h in range(H):
+        for o in (1, 3, 2):
+            xcp[h, o].wait_recv()
+            vcp[h, o].wait_recv()
+            c_send(c * NX + xo(NX - o), h, o)
+        if h:
+            mm1(h - 1)
+    mm1(H - 1)
 
     for start, size in ((0, 128), (128, 128), (MAIN, OV)):
         r = slice(start, start + size)
@@ -335,9 +340,8 @@
 
     c2, x2, z2, y2 = {}, {}, {}, {}
 
-    def mm2(i):
-        n = slice(i * 1024, (i + 1) * 1024)
-        obf[:, n] = jnp.dot(p_v[...], e_v[:, n], preferred_element_type=F32).astype(BF16)
+    def mm2(h):
+        obf[:, cols(h)] = jnp.dot(p_v[...], e_v[:, cols(h)], preferred_element_type=F32).astype(BF16)
 
     def core_send(h):
         src = obf.at[rows((1 - c) * NX * LR, NX * LR), pl.ds(h * DH, DH)]
@@ -357,20 +361,12 @@
     cp.wait_recv()
     loc2 = st_c[0:1]
     cur = merge([cur, got3(st_c)])
+    chip = cur[0]
     put(1, cur)
-    cps = [send(st_o.at[1], st_x.at[o], sxs.at[o], sxr.at[o], xpart(o)) for o in xoffs]
-    mm2(1)
+    xst = [send(st_o.at[1], st_x.at[o], sxs.at[o], sxr.at[o], xpart(o)) for o in xoffs]
     core_send(0)
-    mm2(2)
-    for cp in cps:
-        cp.wait_recv()
-    cur = merge([cur] + [got3(st_x[o]) for o in xoffs])
-    put(2, cur)
-    scp = [send(st_o.at[2], st_z.at[o], szs.at[o], szr.at[o], zpart(o)) for o in zoffs]
-    spread(fsc, jnp.exp(loc - cur[0]))
-    spread(fs2, jnp.exp(loc2 - cur[0]))
-    mm2(3)
-    core_send(1)
+    spread(fsc, jnp.exp(loc - chip))
+    spread(fs2, jnp.exp(loc2 - chip))
 
     def x2_send(h, o, to):
         x2[h, o] = send(xs.at[h, o], xr.at[h, o], x2send.at[h, o], x2recv.at[h, o], xpart(to))
@@ -395,7 +391,7 @@
             theirs = cro[h, rows(xx * OV, OV), sub:sub + 128].astype(F32)
             xs[h, o, MAIN:, sub:sub + 128] = (mine * fa + theirs * fb).astype(BF16)
 
-    for h in range(H):
+    def chip_sums(h):
         c2[h, 0].wait_recv()
         c2[h, 1].wait_recv()
         for o in (2, 1, 3, 0):
@@ -403,17 +399,28 @@
             if o:
                 x2_send(h, o, o)
 
-    for cp in scp:
+    for h in range(1, H):
+        mm2(h)
+        core_send(h)
+        chip_sums(h - 1)
+    chip_sums(H - 1)
+
+    for cp in xst:
         cp.wait_recv()
-    m8 = cur[0]
+    cur = merge([cur] + [got3(st_x[o]) for o in xoffs])
+    put(2, cur)
+    zst = [send(st_o.at[2], st_z.at[o], szs.at[o], szr.at[o], zpart(o)) for o in zoffs]
+    for cp in zst:
+        cp.wait_recv()
     m1, m2, sm = merge([cur] + [got3(st_z[o]) for o in zoffs])
-    spread(fsc, jnp.exp(m8 - m1) / sm * 64.0)
+    for o in range(NX):
+        spread(fx.at[o], jnp.exp((st_x[o, 0:1] if o else chip) - m1) / sm * 64.0)
     margin = (1.0 - jnp.exp(m2 - m1)) / sm
     mg[y] = jnp.broadcast_to(margin, (8, ML))
     mcp = [send(mg.at[y], mg.at[y], ms.at[o], mr.at[o], ypart(o)) for o in yoffs]
 
-    f_main = fsc[rows(line * LR, LR)]
-    f_ov = further_factor(fsc, line)
+    f_main = [fx[o, rows(line * LR, LR)] for o in range(NX)]
+    f_ov = [further_factor(fx.at[o], line) for o in range(NX)]
 
     for h in range(H):
         for o in (1, 3, 2):
@@ -422,9 +429,11 @@
             ln = slice(lane, lane + 128)
             for cc in range(NK + 1):
                 r = slice(cc * LR, min(cc * LR + LR, M))
-                tot = xs[h, 0, r, ln].astype(F32) + xr[h, 1, r, ln].astype(F32)
-                tot = tot + xr[h, 3, r, ln].astype(F32) + xr[h, 2, r, ln].astype(F32)
-                pst[r, ln] = (tot * (f_main if cc < NK else f_ov)).astype(BF16)
+                f = f_main if cc < NK else f_ov
+                tot = xs[h, 0, r, ln].astype(F32) * f[0]
+                for o in xoffs:
+                    tot = tot + xr[h, o, r, ln].astype(F32) * f[o]
+                pst[r, ln] = tot.astype(BF16)
         zs[h] = jnp.dot(perm2[...], pst[...], preferred_element_type=F32).astype(BF16)
         for o in zoffs:
             src = zs.at[h, rows(lax.rem(z + o, NZ) * ROWS, ROWS)]
@@ -531,6 +540,7 @@
             pltpu.VMEM((3, 128, ML), F32),
             pltpu.VMEM((M, 128), F32),
             pltpu.VMEM((M, 128), F32),
+            pltpu.VMEM((NX, M, 128), F32),
             pltpu.VMEM((M, D), BF16),
             pltpu.VMEM((H, NK * OV, CW), BF16),
             pltpu.VMEM((H, NX * LR, DH), BF16),
@@ -566,11 +576,22 @@
     )(q, sc, gain, table, counts, positions)
 
 
+def hand_out(a, b, out_a, out_b):
+    out_a[...] = a[...]
+    out_b[...] = b[...]
+
+
 def on_device(quantized, scales, norm_gain, embed_table, counts, positions):
     expected, margins = readout(
         quantized[0], scales[0], norm_gain.reshape(1, D), embed_table, counts,
         positions.transpose(1, 2, 0),
     )
+    vm = pl.BlockSpec(memory_space=pltpu.VMEM)
+    expected, margins = pl.pallas_call(
+        hand_out,
+        out_shape=tuple(jax.ShapeDtypeStruct(a.shape, a.dtype) for a in (expected, margins)),
+        in_specs=[vm, vm], out_specs=(vm, vm), name="hand_out",
+    )(expected, margins)
     return (expected[None], margins)
 
 

time: 75.3 us -> 66.5 us (0.88)
  Pallas kernels: 71 us -> 65.5 us
  local copies, waits for them, and re-layouts: 2.81 us -> 0 us
    pallas_call x1, Pallas kernels: 71 us -> 63.9 us  [readout(): pl.pallas_call(kernel, out_shape=(jax.ShapeDtypeStruct(q.shape, BF16), ja...]
    unnamed x2 -> x0, local copies, waits for them, and re-layouts: 2.81 us -> none
    pallas_call x0 -> x1, Pallas kernels: none -> 1.53 us  [on_device(): pl.pallas_call(hand_out, out_shape=tuple((jax.ShapeDtypeStruct(a.shape, a...]
where the time goes in v4:
time: 66.5 us; the launch traced here: 66.1 us
  Pallas kernels  65.5 us (98%)
    pallas_call x1, Pallas kernels, readout(): pl.pallas_call(kernel, out_shape=(jax.ShapeDtypeStruct(q.shape, BF16), ja...  63.9 us
    pallas_call x1, Pallas kernels, on_device(): pl.pallas_call(hand_out, out_shape=tuple((jax.ShapeDtypeStruct(a.shape, a...  1.53 us

profile of v4, /device:TPU:16, one launch (start us, length us, event | category | flops | bytes accessed | tf_op | source)
XLA Modules:
  0.0 66.1 jit_solution(6083646555517969586)
XLA Ops:
  0.6 63.9 %readout.1 = (bf16[5,2,4096]{2,1,0:T(2,128)(2,1)}, f32[2,10]{1,0:T(2,128)}) custom-call(bf16[5,2,4096]{2,1,0:T(2,128)(2,1)} %bitcast.5, f32[5,2,32]{2,1,0:T(2,128)} %bitcast.8, f32[1,4096]{1,0:T(1,128)} %bitcast.7, bf16[1280,4096]{1,0:T(8,128)(2,1)} %e_hbm.1, s32[8]{0:T(128)} %cnt_ref.1, s32[5,2,64]{2,1,0:T(2,128)} %bitcast.9), custom_call_target="tpu_custom_call" | custom-call | flops 5704253440 | bytes 10485760 | tf_op jit(solution)/shard_map/readout/pallas_call | solution.py:514
  64.6 1.5 %hand_out.1 = (bf16[5,2,4096]{2,1,0:T(2,128)(2,1)}, f32[2,10]{1,0:T(2,128)}) custom-call(bf16[5,2,4096]{2,1,0:T(2,128)(2,1)} %get-tuple-element.6.a, f32[2,10]{1,0:T(2,128)} %get-tuple-element.7.b), custom_call_target="tpu_custom_call" | custom-call | tf_op jit(solution)/shard_map/hand_out/pallas_call | solution.py:590

commit v5 on v4

--- a/solution.py
+++ b/solution.py
@@ -31,6 +31,10 @@
 SLOTS = 10
 SP = 16
 BARS = 40
+Y_OUT = ((0, 1), (1, 4))
+Z_OUT = ((0, 1), (1, 2), (2, 3), (3, 4))
+Z_BACK = ((0, 1), (1, 2), (2, 3), (3, 4))
+Y_BACK = ((0, 3), (3, 4))
 
 
 def onehot(cond):
@@ -66,10 +70,9 @@
 def kernel(
     q_ref, sc_ref, gain_ref, e_hbm, cnt_ref, pos_ref,
     out_ref, marg_ref,
-    e_v, qf, sf, xcat, sb, yr, g, perm1, perm2, swap, back, x_v, ov_g, l_v, p_v, tt, fsc, fs2, fx, obf,
-    ovo, cr, cro, xs, xr, pst, zs, zr, ys, yr2, res, mg, st_c, st_x, st_z, st_o,
+    e_v, qf, sf, xcat, sb, yr, g, perm1, perm2, swap, back, x_v, lg, l_v, p_v, tt, fsc, fs2, fx, obf,
+    ovo, cr, cro, xs, xr, pst, zs, zr, yr2, res, mg, st_c, st_x, st_z, st_o,
     esem, ysend, yrecv, zsend, zrecv, xsend, xrecv, csend, crecv,
-    vsend, vrecv, wsend, wrecv,
     c2send, c2recv, x2send, x2recv, z2send, z2recv, y2send, y2recv,
     scs, scr, sxs, sxr, szs, szr, ms, mr,
 ):
@@ -180,14 +183,15 @@
     for h in range(H):
         blocks = jnp.dot(pick, xcat[h], preferred_element_type=F32).astype(BF16)
         for o in range(NY):
-            sb[h, o] = blocks[o * ROWS:(o + 1) * ROWS]
+            sb[o, h] = blocks[o * ROWS:(o + 1) * ROWS]
 
     pl.semaphore_wait(barrier, len(partners))
 
     ycp = {}
-    for h in range(H):
+    for a, b in Y_OUT:
         for o in yoffs:
-            ycp[h, o] = send(sb.at[h, o], yr.at[h, o], ysend.at[h, o], yrecv.at[h, o], ypart(o))
+            src, dst = sb.at[o, a:b], yr.at[o, a:b]
+            ycp[a, o] = send(src, dst, ysend.at[a, o], yrecv.at[a, o], ypart(o))
 
     def place(i, dim):
         zz = div48(i)
@@ -206,14 +210,17 @@
     zcp = {}
     for h in range(H):
         for o in yoffs:
-            ycp[h, o].wait_recv()
-        own = sb[h, 0].astype(F32)
+            if (h, o) in ycp:
+                ycp[h, o].wait_recv()
+        own = sb[0, h].astype(F32)
         for o in yoffs:
-            own = own + yr[h, o].astype(F32)
+            own = own + yr[o, h].astype(F32)
         g[h, rows(z * ROWS, ROWS), :] = own.astype(BF16)
-        for o in zoffs:
-            mine = g.at[h, rows(z * ROWS, ROWS)]
-            zcp[h, o] = send(mine, mine, zsend.at[h, o], zrecv.at[h, o], zpart(o))
+        for a, b in Z_OUT:
+            if b == h + 1:
+                mine = g.at[a:b, rows(z * ROWS, ROWS)]
+                for o in zoffs:
+                    zcp[a, o] = send(mine, mine, zsend.at[a, o], zrecv.at[a, o], zpart(o))
 
     si = iota((128, 1), 0)
     sa, sbb = lax.shift_right_logical(si, 4), jnp.bitwise_and(lax.shift_right_logical(si, 1), 7)
@@ -237,41 +244,24 @@
         & (jnp.broadcast_to(code_i, shape) == jnp.broadcast_to(have, shape))
     )
 
-    xcp, ccp, vcp, wcp = {}, {}, {}, {}
-
-    def main_at(ln, h):
-        return x_v.at[rows(ln * LR, LR), pl.ds(h * DH, DH)]
-
-    def further_at(ln, h):
-        return ov_g.at[h, rows(ln * OV, OV)]
-
-    def x_send(ln, h, o, to):
-        a, b = main_at(ln, h), further_at(ln, h)
-        xcp[h, o] = send(a, a, xsend.at[h, o], xrecv.at[h, o], to)
-        vcp[h, o] = send(b, b, vsend.at[h, o], vrecv.at[h, o], to)
-
-    def c_send(ln, h, o):
-        a, b = main_at(ln, h), further_at(ln, h)
-        ccp[h, o] = send(a, a, csend.at[h, o], crecv.at[h, o], cpart)
-        wcp[h, o] = send(b, b, wsend.at[h, o], wrecv.at[h, o], cpart)
-
+    xcp, ccp = {}, {}
     for h in range(H):
         for o in zoffs:
-            zcp[h, o].wait_recv()
-        lines = jnp.dot(perm1[...], g[h], preferred_element_type=F32).astype(BF16)
-        for cc in range(NK):
-            ln = slice(h * DH + cc * CW, h * DH + (cc + 1) * CW)
-            x_v[rows(line * LR, LR), ln] = lines[cc * LR:(cc + 1) * LR]
-        ov_g[h, rows(line * OV, OV)] = lines[MAIN:]
+            if (h, o) in zcp:
+                zcp[h, o].wait_recv()
+        lg[h, line] = jnp.dot(perm1[...], g[h], preferred_element_type=F32).astype(BF16)
+        mine = lg.at[h, line]
         for o in xoffs:
-            x_send(line, h, o, xpart(o))
-        c_send(line, h, 0)
+            xcp[h, o] = send(mine, mine, xsend.at[h, o], xrecv.at[h, o], xpart(o))
 
     def mm1(h):
-        for o in (0, 1, 3, 2):
-            ccp[h, o].wait_recv()
-            wcp[h, o].wait_recv()
-        further = jnp.dot(swap[...], ov_g[h], preferred_element_type=F32).astype(BF16)
+        ccp[h].wait_recv()
+        for ln in range(NK):
+            for cc in range(NK):
+                at = slice(h * DH + cc * CW, h * DH + (cc + 1) * CW)
+                x_v[ln * LR:(ln + 1) * LR, at] = lg[h, ln, cc * LR:(cc + 1) * LR]
+        stack = jnp.concatenate([lg[h, ln, MAIN:] for ln in range(NK)], axis=0)
+        further = jnp.dot(swap[...], stack, preferred_element_type=F32).astype(BF16)
         for cc in range(NK):
             x_v[MAIN:, h * DH + cc * CW:h * DH + (cc + 1) * CW] = further[cc * OV:(cc + 1) * OV]
         if h == 0:
@@ -291,8 +281,8 @@
     for h in range(H):
         for o in (1, 3, 2):
             xcp[h, o].wait_recv()
-            vcp[h, o].wait_recv()
-            c_send(c * NX + xo(NX - o), h, o)
+        mine = lg.at[h, pl.ds(c * NX, NX)]
+        ccp[h] = send(mine, mine, csend.at[h], crecv.at[h], cpart)
         if h:
             mm1(h - 1)
     mm1(H - 1)
@@ -358,13 +348,13 @@
     put(0, cur)
     cp = send(st_o.at[0], st_c, scs, scr, cpart)
     mm2(0)
+    core_send(0)
     cp.wait_recv()
     loc2 = st_c[0:1]
     cur = merge([cur, got3(st_c)])
     chip = cur[0]
     put(1, cur)
     xst = [send(st_o.at[1], st_x.at[o], sxs.at[o], sxr.at[o], xpart(o)) for o in xoffs]
-    core_send(0)
     spread(fsc, jnp.exp(loc - chip))
     spread(fs2, jnp.exp(loc2 - chip))
 
@@ -435,9 +425,12 @@
                     tot = tot + xr[h, o, r, ln].astype(F32) * f[o]
                 pst[r, ln] = tot.astype(BF16)
         zs[h] = jnp.dot(perm2[...], pst[...], preferred_element_type=F32).astype(BF16)
-        for o in zoffs:
-            src = zs.at[h, rows(lax.rem(z + o, NZ) * ROWS, ROWS)]
-            z2[h, o] = send(src, zr.at[h, o], z2send.at[h, o], z2recv.at[h, o], zpart(o))
+        for a, b in Z_BACK:
+            if b == h + 1:
+                for o in zoffs:
+                    src = zs.at[a:b, rows(lax.rem(z + o, NZ) * ROWS, ROWS)]
+                    dst = zr.at[o, a:b]
+                    z2[a, o] = send(src, dst, z2send.at[a, o], z2recv.at[a, o], zpart(o))
 
     for cp in mcp:
         cp.wait_recv()
@@ -486,19 +479,23 @@
 
     for h in range(H):
         for o in zoffs:
-            z2[h, o].wait_recv()
+            if (h, o) in z2:
+                z2[h, o].wait_recv()
         tot = zs[h, rows(z * ROWS, ROWS), :].astype(F32)
         for o in zoffs:
-            tot = tot + zr[h, o].astype(F32)
-        ys[h] = tot.astype(BF16)
-        yr2[h, 0] = ys[h]
-        for o in yoffs:
-            y2[h, o] = send(ys.at[h], yr2.at[h, o], y2send.at[h, o], y2recv.at[h, o], ypart(o))
+            tot = tot + zr[o, h].astype(F32)
+        yr2[0, h] = tot.astype(BF16)
+        for a, b in Y_BACK:
+            if b == h + 1:
+                for o in yoffs:
+                    src, dst = yr2.at[0, a:b], yr2.at[o, a:b]
+                    y2[a, o] = send(src, dst, y2send.at[a, o], y2recv.at[a, o], ypart(o))
 
     for h in range(H):
         for o in yoffs:
-            y2[h, o].wait_recv()
-        cat = jnp.concatenate([yr2[h, o] for o in range(NY)], axis=0)
+            if (h, o) in y2:
+                y2[h, o].wait_recv()
+        cat = jnp.concatenate([yr2[o, h] for o in range(NY)], axis=0)
         got = jnp.dot(back[...], cat, preferred_element_type=F32)
         for cc in range(NK):
             res[:, h * DH + cc * CW:h * DH + (cc + 1) * CW] = got[cc * SP:(cc + 1) * SP]
@@ -526,15 +523,15 @@
             pltpu.VMEM((SP, D), F32),
             pltpu.VMEM((SP, D // 128), F32),
             pltpu.VMEM((H, NK * SP, CW), BF16),
-            pltpu.VMEM((H, NY, ROWS, CW), BF16),
-            pltpu.VMEM((H, NY, ROWS, CW), BF16),
+            pltpu.VMEM((NY, H, ROWS, CW), BF16),
+            pltpu.VMEM((NY, H, ROWS, CW), BF16),
             pltpu.VMEM((H, GR, CW), BF16),
             pltpu.VMEM((M, GR), BF16),
             pltpu.VMEM((GR, M), BF16),
             pltpu.VMEM((128, 128), BF16),
             pltpu.VMEM((NK * SP, NY * ROWS), BF16),
             pltpu.VMEM((M, D), BF16),
-            pltpu.VMEM((H, NK * OV, CW), BF16),
+            pltpu.VMEM((H, NK, M, CW), BF16),
             pltpu.VMEM((M, V), F32),
             pltpu.VMEM((M, V), BF16),
             pltpu.VMEM((3, 128, ML), F32),
@@ -549,9 +546,8 @@
             pltpu.VMEM((H, NX, M, CW), BF16),
             pltpu.VMEM((M, CW), BF16),
             pltpu.VMEM((H, GR, CW), BF16),
-            pltpu.VMEM((H, NZ, ROWS, CW), BF16),
-            pltpu.VMEM((H, ROWS, CW), BF16),
-            pltpu.VMEM((H, NY, ROWS, CW), BF16),
+            pltpu.VMEM((NZ, H, ROWS, CW), BF16),
+            pltpu.VMEM((NY, H, ROWS, CW), BF16),
             pltpu.VMEM((SP, D), F32),
             pltpu.VMEM((NY, 8, ML), F32),
             pltpu.VMEM((8, ML), F32),
@@ -560,8 +556,7 @@
             pltpu.VMEM((3, 8, ML), F32),
             dma,
             dma((H, NY)), dma((H, NY)), dma((H, NZ)), dma((H, NZ)),
-            dma((H, NX)), dma((H, NX)), dma((H, NX)), dma((H, NX)),
-            dma((H, NX)), dma((H, NX)), dma((H, NX)), dma((H, NX)),
+            dma((H, NX)), dma((H, NX)), dma((H,)), dma((H,)),
             dma((H, 2)), dma((H, 2)), dma((H, NX)), dma((H, NX)),
             dma((H, NZ)), dma((H, NZ)), dma((H, NY)), dma((H, NY)),
             dma, dma, dma((NX,)), dma((NX,)), dma((NZ,)), dma((NZ,)), dma((NY,)), dma((NY,)),

time: 66.5 us -> 65.7 us (0.988)
  no operation moved by 1% of the time
where the time goes in v5:
time: 65.7 us; the launch traced here: 65.5 us
  Pallas kernels  64.9 us (99%)
    pallas_call x1, Pallas kernels, readout(): pl.pallas_call(kernel, out_shape=(jax.ShapeDtypeStruct(q.shape, BF16), ja...  63.4 us
    pallas_call x1, Pallas kernels, on_device(): pl.pallas_call(hand_out, out_shape=tuple((jax.ShapeDtypeStruct(a.shape, a...  1.53 us

profile of v5, /device:TPU:16, one launch (start us, length us, event | category | flops | bytes accessed | tf_op | source)
XLA Modules:
  0.0 65.5 jit_solution(15188098953741572361)
XLA Ops:
  0.6 63.4 %readout.1 = (bf16[5,2,4096]{2,1,0:T(2,128)(2,1)}, f32[2,10]{1,0:T(2,128)}) custom-call(bf16[5,2,4096]{2,1,0:T(2,128)(2,1)} %bitcast.5, f32[5,2,32]{2,1,0:T(2,128)} %bitcast.8, f32[1,4096]{1,0:T(1,128)} %bitcast.7, bf16[1280,4096]{1,0:T(8,128)(2,1)} %e_hbm.1, s32[8]{0:T(128)} %cnt_ref.1, s32[5,2,64]{2,1,0:T(2,128)} %bitcast.9), custom_call_target="tpu_custom_call" | custom-call | flops 5704253440 | bytes 10485760 | tf_op jit(solution)/shard_map/readout/pallas_call | solution.py:511
  64.0 1.5 %hand_out.1 = (bf16[5,2,4096]{2,1,0:T(2,128)(2,1)}, f32[2,10]{1,0:T(2,128)}) custom-call(bf16[5,2,4096]{2,1,0:T(2,128)(2,1)} %get-tuple-element.6.a, f32[2,10]{1,0:T(2,128)} %get-tuple-element.7.b), custom_call_target="tpu_custom_call" | custom-call | tf_op jit(solution)/shard_map/hand_out/pallas_call | solution.py:585

commit v6 on v5

--- a/solution.py
+++ b/solution.py
@@ -31,10 +31,10 @@
 SLOTS = 10
 SP = 16
 BARS = 40
-Y_OUT = ((0, 1), (1, 4))
+Y_OUT = ((0, 1), (1, 2), (2, 3), (3, 4))
 Z_OUT = ((0, 1), (1, 2), (2, 3), (3, 4))
 Z_BACK = ((0, 1), (1, 2), (2, 3), (3, 4))
-Y_BACK = ((0, 3), (3, 4))
+Y_BACK = ((0, 1), (1, 2), (2, 3), (3, 4))
 
 
 def onehot(cond):
@@ -110,6 +110,13 @@
         cp.start()
         pending.append(cp)
         return cp
+
+    def drain(keep=()):
+        kept = [cp for cp in pending if any(cp is k for k in keep)]
+        for cp in pending:
+            if not any(cp is k for k in keep):
+                cp.wait_send()
+        pending[:] = kept
 
     def rows(start, size):
         return pl.ds(pl.multiple_of(start, 16), size)
@@ -267,16 +274,11 @@
         if h == 0:
             e_copy.wait()
 
-        def body(i, carry):
-            n = pl.ds(pl.multiple_of(i * 640, 640), 640)
-            part = lax.dot_general(
-                x_v[:, cols(h)], e_v[n, cols(h)],
-                (((1,), (1,)), ((), ())), preferred_element_type=F32,
-            )
-            l_v[:, n] = part if h == 0 else l_v[:, n] + part
-            return carry
-
-        lax.fori_loop(0, V // 640, body, 0)
+        part = lax.dot_general(
+            x_v[:, cols(h)], e_v[:, cols(h)],
+            (((1,), (1,)), ((), ())), preferred_element_type=F32,
+        )
+        l_v[...] = part if h == 0 else l_v[...] + part
 
     for h in range(H):
         for o in (1, 3, 2):
@@ -409,6 +411,7 @@
     mg[y] = jnp.broadcast_to(margin, (8, ML))
     mcp = [send(mg.at[y], mg.at[y], ms.at[o], mr.at[o], ypart(o)) for o in yoffs]
 
+    drain(list(x2.values()) + mcp)
     f_main = [fx[o, rows(line * LR, LR)] for o in range(NX)]
     f_ov = [further_factor(fx.at[o], line) for o in range(NX)]
 
@@ -432,6 +435,7 @@
                     dst = zr.at[o, a:b]
                     z2[a, o] = send(src, dst, z2send.at[a, o], z2recv.at[a, o], zpart(o))
 
+    drain(list(z2.values()) + mcp)
     for cp in mcp:
         cp.wait_recv()
     lane = iota((1, ML), 1)
@@ -491,6 +495,7 @@
                     src, dst = yr2.at[0, a:b], yr2.at[o, a:b]
                     y2[a, o] = send(src, dst, y2send.at[a, o], y2recv.at[a, o], ypart(o))
 
+    drain(y2.values())
     for h in range(H):
         for o in yoffs:
             if (h, o) in y2:
@@ -501,8 +506,7 @@
             res[:, h * DH + cc * CW:h * DH + (cc + 1) * CW] = got[cc * SP:(cc + 1) * SP]
     for i in range(5):
         out_ref[i] = res[2 * i:2 * i + 2].astype(BF16)
-    for cp in pending:
-        cp.wait_send()
+    drain()
 
 
 def readout(q, sc, gain, table, counts, positions):

time: 65.7 us -> 65.9 us (level); the launches traced: 65.5 us -> 64.8 us
  Pallas kernels: 64.9 us -> 64.1 us
    pallas_call x1, Pallas kernels: 63.4 us -> 62.6 us  [readout(): pl.pallas_call(kernel, out_shape=(jax.ShapeDtypeStruct(q.shape, BF16), ja...]
where the time goes in v6:
time: 65.9 us; the launch traced here: 64.8 us
  Pallas kernels  64.1 us (97%)
    pallas_call x1, Pallas kernels, readout(): pl.pallas_call(kernel, out_shape=(jax.ShapeDtypeStruct(q.shape, BF16), ja...  62.6 us
    pallas_call x1, Pallas kernels, on_device(): pl.pallas_call(hand_out, out_shape=tuple((jax.ShapeDtypeStruct(a.shape, a...  1.53 us

profile of v6, /device:TPU:16, one launch (start us, length us, event | category | flops | bytes accessed | tf_op | source)
XLA Modules:
  0.0 64.8 jit_solution(1109797852923760770)
XLA Ops:
  0.6 62.6 %readout.1 = (bf16[5,2,4096]{2,1,0:T(2,128)(2,1)}, f32[2,10]{1,0:T(2,128)}) custom-call(bf16[5,2,4096]{2,1,0:T(2,128)(2,1)} %bitcast.5, f32[5,2,32]{2,1,0:T(2,128)} %bitcast.8, f32[1,4096]{1,0:T(1,128)} %bitcast.7, bf16[1280,4096]{1,0:T(8,128)(2,1)} %e_hbm.1, s32[8]{0:T(128)} %cnt_ref.1, s32[5,2,64]{2,1,0:T(2,128)} %bitcast.9), custom_call_target="tpu_custom_call" | custom-call | flops 5704253440 | bytes 10485760 | tf_op jit(solution)/shard_map/readout/pallas_call | solution.py:515
  63.2 1.5 %hand_out.1 = (bf16[5,2,4096]{2,1,0:T(2,128)(2,1)}, f32[2,10]{1,0:T(2,128)}) custom-call(bf16[5,2,4096]{2,1,0:T(2,128)(2,1)} %get-tuple-element.6.a, f32[2,10]{1,0:T(2,128)} %get-tuple-element.7.b), custom_call_target="tpu_custom_call" | custom-call | tf_op jit(solution)/shard_map/hand_out/pallas_call | solution.py:589
